TPU v7x, 32 devices: a whole 2x2x4 slice. The times are simulated.
32 devices in a mesh: seq: 8 (over z, y), head: 4 (over x, core).
Axes of the slice: x: 2, y: 2, z: 4, core: 2. Of those that a mesh axis runs over, the one named last changes fastest.
Arguments:
- tokens: bfloat16 [16384, 512], P(('seq', 'head')), may hold values from -6 to 6
- lengths: int32 [3], replicated, may hold values from 512 to 14336, as said below
- feature_seed: int32 [1], replicated, may hold values from 0 to 1048575
- norm_gain: bfloat16 [512], P('seq'), may hold values from 0.5 to 1.5
- norm_shift: bfloat16 [512], P('seq'), may hold values from -1.5 to 1.5
- query_weight: bfloat16 [512, 512], P('seq', 'head'), may hold values from -0.25 to 0.25
- key_weight: bfloat16 [512, 512], P('seq', 'head'), may hold values from -0.25 to 0.25
- value_weight: bfloat16 [512, 512], P('seq', 'head'), may hold values from -0.25 to 0.25
- gate_weight: bfloat16 [512, 8], P('seq', 'head'), may hold values from -0.25 to 0.25
- gate_bias: float32 [8], P('head'), may hold values from 3.5 to 14
- out_weight: bfloat16 [512, 512], P('head', 'seq'), may hold values from -0.75 to 0.75
- ffn_gain: bfloat16 [512], P('seq'), may hold values from 0.5 to 1.5
- ffn_shift: bfloat16 [512], P('seq'), may hold values from -1.5 to 1.5
- up_weight: bfloat16 [512, 2048], P('seq', 'head'), may hold values from -0.25 to 0.25
- down_weight: bfloat16 [2048, 512], P('head', 'seq'), may hold values from -0.125 to 0.125
- cotangent: bfloat16 [16384, 512], P(('seq', 'head')), may hold values from -6 to 6
Outputs:
- result: bfloat16 [16384, 512], P(('seq', 'head'))
- grad_tokens: float32 [16384, 512], P(('seq', 'head'))
- grad_norm_gain: float32 [512], P('seq')
- grad_norm_shift: float32 [512], P('seq')
- grad_query_weight: float32 [512, 512], P('seq', 'head')
- grad_key_weight: float32 [512, 512], P('seq', 'head')
- grad_value_weight: float32 [512, 512], P('seq', 'head')
- grad_gate_weight: float32 [512, 8], P('seq', 'head')
- grad_gate_bias: float32 [8], P('head')
- grad_out_weight: float32 [512, 512], P('head', 'seq')
- grad_ffn_gain: float32 [512], P('seq')
- grad_ffn_shift: float32 [512], P('seq')
- grad_up_weight: float32 [512, 2048], P('seq', 'head')
- grad_down_weight: float32 [2048, 512], P('head', 'seq')
Inputs may be any that keep to these rules, and one draw needn't show every extreme that they name: `lengths`: the documents lie end to end from the first token; the tokens from filled on are padding, at least two. Two entries are sentences of 512 to 1023 tokens; the other, second or third in the list, is one document of exactly 14336 tokens, which begins among the first 2048 tokens and ends among the last 2048.
All inputs are finite; a program needn't handle non-finite values.
Results may differ from a plain program's by a relative error of at most 0.02.
The roundings to bfloat16 on the way count: a program that leaves them out, or rounds other values in their place, can miss the bound.
Values may be sent and summed in bfloat16 or wider, within the bound.
A program may use at most 128 MiB of HBM per device.

v0:
```python
import math

import jax
import jax.numpy as jnp
from jax import lax
from jax.sharding import PartitionSpec as P

HEADS = 8
HEAD_DIM = 64
FEATS = 128


eps = 1e-05
den_floor = 0.25
gate_pen = 0.5
highest = lax.Precision.HIGHEST


def carried_in(part, axis, combine, identity, reverse):
    count = lax.axis_size(axis)
    place = lax.axis_index(axis)
    ahead = count - 1 - place if reverse else place
    gathered = jax.tree.map(lambda a: lax.all_gather(a, axis), part)
    state = jax.tree.map(lambda a, e: jnp.zeros_like(a) + jnp.asarray(e, a.dtype), part, identity)

    def one(lap, state):
        source = count - 1 - lap if reverse else lap
        return combine(
            state, jax.tree.map(lambda a: lax.dynamic_index_in_dim(a, source, 0, False), gathered)
        )

    return lax.fori_loop(0, ahead, one, state)


def narrowed(values):
    return values + lax.stop_gradient(values.astype(jnp.bfloat16).astype(jnp.float32) - values)


def gauss_table(feature_seed, entries):
    positions = jnp.arange(entries, dtype=jnp.int32)
    hashed = positions * jnp.int32(-1640531535) + feature_seed[0] * jnp.int32(-2048144789)
    hashed = hashed ^ lax.shift_right_logical(hashed, jnp.int32(15))
    hashed = hashed * jnp.int32(739982445)
    hashed = hashed ^ lax.shift_right_logical(hashed, jnp.int32(13))
    hashed = hashed * jnp.int32(695872825)
    hashed = hashed ^ lax.shift_right_logical(hashed, jnp.int32(16))
    summed = jnp.zeros((entries,), jnp.int32)
    for shift_step in range(4):
        summed = summed + (
            lax.shift_right_logical(hashed, jnp.int32(8 * shift_step)) & jnp.int32(255)
        )
    return (summed.astype(jnp.float32) - 510.0) / math.sqrt(21845.0)


def norm_parts(values):
    center = jnp.mean(values, axis=-1, keepdims=True)
    spread = jnp.mean(values * values, axis=-1, keepdims=True) - center * center
    inv_std = lax.rsqrt(spread + eps)
    return ((values - center) * inv_std, inv_std)


def norm_backward(grad_out, centered, inv_std, gain):
    scaled_grad = grad_out * gain
    return inv_std * (
        scaled_grad
        - jnp.mean(scaled_grad, axis=-1, keepdims=True)
        - centered * jnp.mean(scaled_grad * centered, axis=-1, keepdims=True)
    )


def features(vectors, table):
    scaled = vectors * lax.rsqrt(jnp.sum(vectors * vectors, axis=-1, keepdims=True) + 1e-06)
    angles = jnp.einsum("nhe,hef->nhf", scaled, table, precision=highest)
    return jnp.concatenate([jnp.sin(angles), jnp.cos(angles)], axis=-1) / math.sqrt(table.shape[-1])


def token_marks(lengths, offset, amount):
    positions = offset + jnp.arange(amount, dtype=jnp.int32)
    starts = jnp.cumsum(lengths) - lengths
    filled = jnp.sum(lengths)
    segment = jnp.sum((positions[:, None] >= starts[None, :]).astype(jnp.int32), axis=1) + (
        positions >= filled
    ).astype(jnp.int32)
    resets = jnp.any(positions[:, None] == starts[None, :], axis=1).astype(jnp.int32)
    live_mask = (positions < filled).astype(jnp.float32)
    return (segment, resets, live_mask)


def block_step(state_pair, inputs):
    memory, normal = state_pair
    query_feat, key_feat, values, log_decay, segment, resets, live_mask = inputs
    block_len = log_decay.shape[0]
    log_run = jnp.cumsum(log_decay, axis=0)
    carry_flag = (jnp.cumsum(resets) == 0).astype(jnp.float32)
    log_gap = jnp.minimum(log_run[:, None, :] - log_run[None, :, :], 0.0)
    places = jnp.arange(block_len)
    linked = ((segment[:, None] == segment[None, :]) & (places[None, :] <= places[:, None])).astype(
        jnp.float32
    )
    weights = (
        jnp.einsum("ihm,shm->ish", query_feat, key_feat, precision=highest)
        * jnp.exp(log_gap)
        * (linked * live_mask[None, :])[:, :, None]
    )
    carried = jnp.exp(log_run) * carry_flag[:, None]
    numerator = jnp.einsum("ish,she->ihe", narrowed(weights), values, precision=highest)
    numerator = numerator + carried[:, :, None] * jnp.einsum(
        "ihm,hme->ihe", query_feat, memory, precision=highest
    )
    norm_sum = jnp.sum(weights, axis=1) + carried * jnp.einsum(
        "ihm,hm->ih", query_feat, normal, precision=highest
    )
    to_end = (
        jnp.exp(log_run[-1][None, :] - log_run)
        * ((segment == segment[-1]).astype(jnp.float32) * live_mask)[:, None]
    )
    memory = carried[-1][:, None, None] * memory + jnp.einsum(
        "shm,she->hme", narrowed(key_feat * to_end[:, :, None]), values, precision=highest
    )
    normal = carried[-1][:, None] * normal + jnp.einsum(
        "shm,sh->hm", key_feat, to_end, precision=highest
    )
    return ((memory, normal), (numerator, norm_sum))


def attention_part(query_f, key_f, value_f, logits, table, segment, resets, live_mask):
    rows_all = logits.shape[0]
    local_heads = logits.shape[1]
    head_dim = table.shape[1]
    query_feat = narrowed(features(query_f.reshape(rows_all, local_heads, head_dim), table))
    key_feat = narrowed(features(key_f.reshape(rows_all, local_heads, head_dim), table))
    values = value_f.reshape(rows_all, local_heads, head_dim)
    log_decay = -jax.nn.softplus(-logits) * (live_mask * (1 - resets))[:, None]
    carry_weight = (
        jnp.exp(jnp.cumsum(log_decay, axis=0))
        * (jnp.cumsum(resets) == 0).astype(jnp.float32)[:, None]
    )
    block_len = min(512, rows_all)
    blocks = rows_all // block_len

    def blocked(array):
        return array.reshape((blocks, block_len) + array.shape[1:])

    start = (
        jnp.zeros((local_heads, table.shape[2] * 2, head_dim), jnp.float32),
        jnp.zeros((local_heads, table.shape[2] * 2), jnp.float32),
    )
    xs = (
        blocked(query_feat),
        blocked(key_feat),
        blocked(values),
        blocked(log_decay),
        blocked(segment),
        blocked(resets),
        blocked(live_mask),
    )
    final_pair, (numerator, norm_sum) = lax.scan(jax.checkpoint(block_step), start, xs)
    numerator = numerator.reshape(rows_all, local_heads, head_dim)
    norm_sum = norm_sum.reshape(rows_all, local_heads)
    return (query_feat, numerator, norm_sum, carry_weight, final_pair[0], final_pair[1])


def join_part(numerator, norm_sum, carry_weight, query_feat, memory_in, normal_in, live_mask):
    numerator = numerator + carry_weight[:, :, None] * jnp.einsum(
        "ihm,hme->ihe", query_feat, memory_in, precision=highest
    )
    norm_sum = norm_sum + carry_weight * jnp.einsum(
        "ihm,hm->ih", query_feat, normal_in, precision=highest
    )
    return (
        live_mask[:, None, None]
        * numerator
        / jnp.sqrt(norm_sum * norm_sum + den_floor**2)[:, :, None]
    )


def chain_forward(earlier, later):
    return (
        earlier[0] * later[0],
        later[0][:, None, None] * earlier[1] + later[1],
        later[0][:, None] * earlier[2] + later[2],
    )


def chain_backward(earlier, later):
    return (
        later[0] * earlier[0],
        later[1] + later[0][:, None, None] * earlier[1],
        later[2] + later[0][:, None] * earlier[2],
    )


def partial_gelu(hidden):
    return jax.nn.gelu(hidden, approximate=False)


def shards(
    tokens,
    lengths,
    feature_seed,
    norm_gain,
    norm_shift,
    query_weight,
    key_weight,
    value_weight,
    gate_weight,
    gate_bias,
    out_weight,
    ffn_gain,
    ffn_shift,
    up_weight,
    down_weight,
    cotangent,
):
    seq_count = lax.axis_size("seq")
    head_place = lax.axis_index("head")
    seq_place = lax.axis_index("seq")
    row_share = tokens.shape[0]
    local_heads = gate_bias.shape[0]
    full_tokens, full_cot = (
        lax.all_gather(tokens, "head", axis=0, tiled=True),
        lax.all_gather(cotangent, "head", axis=0, tiled=True),
    )
    rows_dev = full_tokens.shape[0]
    full_query, full_key, full_value, full_gate, full_out, full_gain, full_shift = (
        lax.all_gather(query_weight, "seq", axis=0, tiled=True),
        lax.all_gather(key_weight, "seq", axis=0, tiled=True),
        lax.all_gather(value_weight, "seq", axis=0, tiled=True),
        lax.all_gather(gate_weight, "seq", axis=0, tiled=True),
        lax.all_gather(out_weight, "seq", axis=1, tiled=True),
        lax.all_gather(norm_gain, "seq", axis=0, tiled=True),
        lax.all_gather(norm_shift, "seq", axis=0, tiled=True),
    )
    full_up, full_down, full_gain_two, full_shift_two = (
        lax.all_gather(up_weight, "seq", axis=0, tiled=True),
        lax.all_gather(down_weight, "seq", axis=1, tiled=True),
        lax.all_gather(ffn_gain, "seq", axis=0, tiled=True),
        lax.all_gather(ffn_shift, "seq", axis=0, tiled=True),
    )
    table = gauss_table(feature_seed, HEADS * HEAD_DIM * FEATS).reshape(HEADS, HEAD_DIM, FEATS)
    table = lax.dynamic_slice_in_dim(table, head_place * local_heads, local_heads, 0)
    segment, resets, live_mask = token_marks(lengths, seq_place * rows_dev, rows_dev)
    pen_scale = gate_pen * (rows_dev * seq_count) / jnp.sum(lengths).astype(jnp.float32)
    gain_one = full_gain.astype(jnp.float32)
    gain_two = full_gain_two.astype(jnp.float32)
    tokens_f = full_tokens.astype(jnp.float32)
    centered_one, inv_one = norm_parts(tokens_f)
    normed = (centered_one * gain_one + full_shift.astype(jnp.float32)).astype(jnp.bfloat16)
    queries = jnp.dot(normed, full_query, preferred_element_type=jnp.float32).astype(jnp.bfloat16)
    keys_all = jnp.dot(normed, full_key, preferred_element_type=jnp.float32).astype(jnp.bfloat16)
    values = jnp.dot(normed, full_value, preferred_element_type=jnp.float32).astype(jnp.bfloat16)
    logits = jnp.dot(normed, full_gate, preferred_element_type=jnp.float32) + gate_bias

    def local_part(query_f, key_f, value_f, gate_logits):
        return attention_part(
            query_f, key_f, value_f, gate_logits, table, segment, resets, live_mask
        )

    part_out, part_back = jax.vjp(
        local_part,
        queries.astype(jnp.float32),
        keys_all.astype(jnp.float32),
        values.astype(jnp.float32),
        logits,
    )
    query_feat, numer_loc, sum_loc, carry_weight, memory_loc, normal_loc = part_out
    stretch_decay = carry_weight[-1]
    prefix_out = carried_in(
        (stretch_decay, memory_loc, normal_loc),
        "seq",
        chain_forward,
        (jnp.ones_like(stretch_decay), jnp.zeros_like(memory_loc), jnp.zeros_like(normal_loc)),
        False,
    )
    memory_in, normal_in = (prefix_out[1], prefix_out[2])

    def joined_part(numerator, norm_sum, weight_run, feat, memory, normal):
        return join_part(numerator, norm_sum, weight_run, feat, memory, normal, live_mask)

    joined, join_back = jax.vjp(
        joined_part, numer_loc, sum_loc, carry_weight, query_feat, memory_in, normal_in
    )
    attended = joined.reshape(rows_dev, local_heads * HEAD_DIM).astype(jnp.bfloat16)
    branch = lax.psum(jnp.dot(attended, full_out, preferred_element_type=jnp.float32), "head")
    middle = tokens_f + branch
    centered_two, inv_two = norm_parts(middle)
    normed_two = (centered_two * gain_two + full_shift_two.astype(jnp.float32)).astype(jnp.bfloat16)
    hidden = jnp.dot(normed_two, full_up, preferred_element_type=jnp.float32)
    gelu_value, gelu_back = jax.vjp(partial_gelu, hidden)
    active = gelu_value.astype(jnp.bfloat16)
    ffn_own = lax.psum_scatter(
        jnp.dot(active, full_down, preferred_element_type=jnp.float32).astype(jnp.bfloat16),
        "head",
        scatter_dimension=0,
        tiled=True,
    ).astype(jnp.float32)
    middle_own = lax.dynamic_slice_in_dim(middle, head_place * row_share, row_share, 0)
    result = (middle_own + ffn_own).astype(jnp.bfloat16)
    grad_active = jnp.dot(full_cot, full_down.T, preferred_element_type=jnp.float32)
    grad_hidden = gelu_back(grad_active)[0].astype(jnp.bfloat16)
    grad_up = jnp.dot(normed_two.T, grad_hidden, preferred_element_type=jnp.float32)
    grad_down = jnp.dot(active.T, full_cot, preferred_element_type=jnp.float32)
    grad_normed_two = lax.psum(
        jnp.dot(grad_hidden, full_up.T, preferred_element_type=jnp.float32), "head"
    )
    grad_gain_two = jnp.sum(grad_normed_two * centered_two, axis=0)
    grad_shift_two = jnp.sum(grad_normed_two, axis=0)
    grad_middle = full_cot.astype(jnp.float32) + norm_backward(
        grad_normed_two, centered_two, inv_two, gain_two
    )
    grad_branch = grad_middle.astype(jnp.bfloat16)
    grad_out = jnp.dot(attended.T, grad_branch, preferred_element_type=jnp.float32)
    grad_attended = jnp.dot(grad_branch, full_out.T, preferred_element_type=jnp.float32).astype(
        jnp.bfloat16
    )
    grad_attended = grad_attended.astype(jnp.float32).reshape(rows_dev, local_heads, HEAD_DIM)
    grad_numer, grad_sum, grad_weight, grad_feat, grad_memory, grad_normal = join_back(
        grad_attended
    )
    suffix_out = carried_in(
        (stretch_decay, grad_memory, grad_normal),
        "seq",
        chain_backward,
        (jnp.ones_like(stretch_decay), jnp.zeros_like(grad_memory), jnp.zeros_like(grad_normal)),
        True,
    )
    memory_end, normal_end = (suffix_out[1], suffix_out[2])
    grad_decay = jnp.sum(memory_end * memory_in, axis=(1, 2)) + jnp.sum(
        normal_end * normal_in, axis=1
    )
    grad_weight = grad_weight.at[-1].add(grad_decay)
    grad_query, grad_key, grad_value, grad_logits = part_back(
        (grad_feat, grad_numer, grad_sum, grad_weight, memory_end, normal_end)
    )
    gate_value = jax.nn.sigmoid(logits)
    grad_logits = (
        grad_logits + pen_scale / HEADS * gate_value * (1.0 - gate_value) * live_mask[:, None]
    )
    grad_query_b = grad_query.astype(jnp.bfloat16)
    grad_key_b = grad_key.astype(jnp.bfloat16)
    grad_value_b = grad_value.astype(jnp.bfloat16)
    grad_normed = jnp.dot(grad_query_b, full_query.T, preferred_element_type=jnp.float32)
    grad_normed = grad_normed + jnp.dot(grad_key_b, full_key.T, preferred_element_type=jnp.float32)
    grad_normed = grad_normed + jnp.dot(
        grad_value_b, full_value.T, preferred_element_type=jnp.float32
    )
    grad_normed = grad_normed + jnp.dot(
        grad_logits, full_gate.astype(jnp.float32).T, precision=highest
    )
    grad_normed = lax.psum(grad_normed.astype(jnp.bfloat16), "head").astype(jnp.float32)
    grad_gain_one = jnp.sum(grad_normed * centered_one, axis=0)
    grad_shift_one = jnp.sum(grad_normed, axis=0)
    grad_tokens_all = grad_middle + norm_backward(grad_normed, centered_one, inv_one, gain_one)
    grad_tokens = lax.dynamic_slice_in_dim(grad_tokens_all, head_place * row_share, row_share, 0)
    grad_query_w = jnp.dot(normed.T, grad_query_b, preferred_element_type=jnp.float32)
    grad_key_w = jnp.dot(normed.T, grad_key_b, preferred_element_type=jnp.float32)
    grad_value_w = jnp.dot(normed.T, grad_value_b, preferred_element_type=jnp.float32)
    grad_gate_w = jnp.dot(normed.astype(jnp.float32).T, grad_logits, precision=highest)
    bias_tile = jnp.broadcast_to(jnp.sum(grad_logits, axis=0)[None, :], (seq_count, local_heads))
    summed_attn = (
        lax.psum_scatter(grad_query_w, "seq", scatter_dimension=0, tiled=True),
        lax.psum_scatter(grad_key_w, "seq", scatter_dimension=0, tiled=True),
        lax.psum_scatter(grad_value_w, "seq", scatter_dimension=0, tiled=True),
        lax.psum_scatter(grad_gate_w, "seq", scatter_dimension=0, tiled=True),
        lax.psum_scatter(grad_out, "seq", scatter_dimension=1, tiled=True),
        lax.psum_scatter(grad_gain_one, "seq", scatter_dimension=0, tiled=True),
        lax.psum_scatter(grad_shift_one, "seq", scatter_dimension=0, tiled=True),
        lax.psum_scatter(bias_tile, "seq", scatter_dimension=0, tiled=True),
    )
    summed_ffn = (
        lax.psum_scatter(
            grad_up.astype(jnp.bfloat16), "seq", scatter_dimension=0, tiled=True
        ).astype(jnp.float32),
        lax.psum_scatter(
            grad_down.astype(jnp.bfloat16), "seq", scatter_dimension=1, tiled=True
        ).astype(jnp.float32),
        lax.psum_scatter(
            grad_gain_two.astype(jnp.bfloat16), "seq", scatter_dimension=0, tiled=True
        ).astype(jnp.float32),
        lax.psum_scatter(
            grad_shift_two.astype(jnp.bfloat16), "seq", scatter_dimension=0, tiled=True
        ).astype(jnp.float32),
    )
    return (
        result,
        grad_tokens,
        summed_attn[5],
        summed_attn[6],
        summed_attn[0],
        summed_attn[1],
        summed_attn[2],
        summed_attn[3],
        summed_attn[7].reshape(local_heads),
        summed_attn[4],
        summed_ffn[2],
        summed_ffn[3],
        summed_ffn[0],
        summed_ffn[1],
    )


def solution(mesh):
    return jax.shard_map(
        shards,
        mesh=mesh,
        in_specs=(
            P(("seq", "head"), None),
            P(),
            P(),
            P("seq"),
            P("seq"),
            P("seq", "head"),
            P("seq", "head"),
            P("seq", "head"),
            P("seq", "head"),
            P("head"),
            P("head", "seq"),
            P("seq"),
            P("seq"),
            P("seq", "head"),
            P("head", "seq"),
            P(("seq", "head"), None),
        ),
        out_specs=(
            P(("seq", "head"), None),
            P(("seq", "head"), None),
            P("seq"),
            P("seq"),
            P("seq", "head"),
            P("seq", "head"),
            P("seq", "head"),
            P("seq", "head"),
            P("head"),
            P("head", "seq"),
            P("seq"),
            P("seq"),
            P("seq", "head"),
            P("head", "seq"),
        ),
        check_vma=False,
    )
```

profile of v0, /device:TPU:0, one launch (start us, length us, event | category | flops | bytes accessed | tf_op | source)
XLA Modules:
  0.0 1490.3 jit_solution(12948245114024279748)
XLA Ops:
  14.2 23.1 %all-reduce.14 = (bf16[512]{0:T(512)(128)(2,1)S(1)}, bf16[512]{0:T(512)(128)(2,1)S(1)}, bf16[512]{0:T(512)(128)(2,1)S(1)}, bf16[512]{0:T(512)(128)(2,1)S(1)}) all-reduce(bf16[512]{0:T(512)(128)(2,1)S(1)} %dynamic-update-slice.4, bf16[512]{0:T(512)(128)(2,1)S(1)} %dynamic-update-slice.3, ...), channel_id=1, replica_groups=mesh['seq'=8,'head'=4] {'seq'}, use_global_device_ids=true, to_apply=%add.4 | all-reduce | flops 2048 | bytes 8192
  37.4 16.4 %all-gather.4 = bf16[8,64,2]{1,2,0:T(2,128)(2,1)S(1)} all-gather(bf16[1,64,2]{1,2,0:T(2,128)(2,1)} %bitcast.840), channel_id=1, replica_groups=mesh['seq'=8,'head'=4] {'seq'}, dimensions={0}, use_global_device_ids=true | all-gather | bytes 2304 | tf_op jit(solution)/shard_map/all_gather | solution.py:229
  56.1 30.8 %all_gather.71 = bf16[512,128]{1,0:T(8,128)(2,1)S(1)} all-gather(bf16[64,128]{1,0:T(8,128)(2,1)} %param.32), channel_id=1, replica_groups=mesh['seq'=8,'head'=4] {'seq'}, dimensions={0}, use_global_device_ids=true | all-gather | bytes 147456 | tf_op jit(solution)/shard_map/all_gather | solution.py:227
  86.8 30.7 %all_gather.72 = bf16[512,128]{1,0:T(8,128)(2,1)S(1)} all-gather(bf16[64,128]{1,0:T(8,128)(2,1)} %param.33), channel_id=1, replica_groups=mesh['seq'=8,'head'=4] {'seq'}, dimensions={0}, use_global_device_ids=true | all-gather | bytes 147456 | tf_op jit(solution)/shard_map/all_gather | solution.py:228
  117.5 32.7 %all_gather.73 = bf16[512,128]{1,0:T(8,128)(2,1)} all-gather(bf16[64,128]{1,0:T(8,128)(2,1)} %param.31), channel_id=1, replica_groups=mesh['seq'=8,'head'=4] {'seq'}, dimensions={0}, use_global_device_ids=true | all-gather | bytes 147456 | tf_op jit(solution)/shard_map/all_gather | solution.py:226
  162.2 8.2 sine_bitcast_fusion.1
  223.3 101.9 %while.79 = (s32[]{:T(128)}, f32[2,256,64]{1,2,0:T(8,128)S(1)}, f32[2,256]{1,0:T(2,128)S(1)}, f32[4,512,2,64]{1,0,3,2:T(4,128)}, f32[4,512,2]{1,2,0:T(2,128)S(1)...) while((s32[]{:T(128)}, f32[2,256,64]{1,2,0:T(8,128)S(1)}, ...), condition=%wide.region_14.15_spmd.clone, body=%wide.region_8.14_spmd.clone.sunk | while | flops 2429790720 | bytes 15763047 | solution.py:157
  326.3 31.0 %all_gather.79 = bf16[128,512]{0,1:T(8,128)(2,1)S(1)} all-gather(bf16[128,64]{0,1:T(8,128)(2,1)S(1)} %copy-done.105), channel_id=1, replica_groups=mesh['seq'=8,'head'=4] {'seq'}, dimensions={1}, use_global_device_ids=true | all-gather | bytes 147456 | tf_op jit(solution)/shard_map/all_gather | solution.py:230
  359.7 17.9 %all-gather.5 = f32[8,1,2]{2,1,0:T(1,128)S(1)} all-gather(f32[1,1,2]{2,1,0:T(1,128)S(1)} %bitcast.841), channel_id=1, replica_groups=mesh['seq'=8,'head'=4] {'seq'}, dimensions={0}, use_global_device_ids=true | all-gather | bytes 72 | tf_op jit(solution)/shard_map/all_gather | solution.py:23
  379.7 26.0 %all-gather.6 = f32[8,2,256]{2,1,0:T(2,128)S(1)} all-gather(f32[1,2,256]{2,1,0:T(2,128)S(1)} %bitcast.815), channel_id=3, replica_groups=mesh['seq'=8,'head'=4] {'seq'}, dimensions={0}, use_global_device_ids=true | all-gather | bytes 18432 | tf_op jit(solution)/shard_map/all_gather | solution.py:23
  419.0 37.2 %all_gather.82 = bf16[512,512]{1,0:T(8,128)(2,1)} all-gather(bf16[64,512]{1,0:T(8,128)(2,1)S(1)} %copy-done.98), channel_id=1, replica_groups=mesh['seq'=8,'head'=4] {'seq'}, dimensions={0}, use_global_device_ids=true | all-gather | bytes 589824 | tf_op jit(solution)/shard_map/all_gather | solution.py:235
  456.2 33.5 %all_gather.83 = bf16[512,512]{0,1:T(8,128)(2,1)} all-gather(bf16[512,64]{0,1:T(8,128)(2,1)} %param.40), channel_id=1, replica_groups=mesh['seq'=8,'head'=4] {'seq'}, dimensions={1}, use_global_device_ids=true | all-gather | bytes 589824 | tf_op jit(solution)/shard_map/all_gather | solution.py:236
  489.7 19.6 %all-reduce.19.cloned.1.call-done = f32[2048,512]{1,0:T(8,128)} async-done(((f32[2048,512]{1,0:T(8,128)}), f32[2048,512]{1,0:T(8,128)}) %all-reduce.19.cloned.1.call-update) | async-done | bytes 4194320 | tf_op jit(solution)/shard_map/psum | solution.py:284
  518.5 15.0 %all-gather.15.cloned.1.call-done = bf16[2048,512]{1,0:T(8,128)(2,1)} async-done(((bf16[512,512]{1,0:T(8,128)(2,1)}), bf16[2048,512]{1,0:T(8,128)(2,1)}) %all-gather.15.cloned.1.call-update) | async-done | bytes 2097168 | tf_op jit(solution)/shard_map/all_gather | solution.py:222
  533.5 13.4 add_convert_fusion.1
  551.6 85.6 %all-reduce.21.cloned.1.call-done = f32[2048,512]{1,0:T(8,128)} async-done(((f32[2048,512]{1,0:T(8,128)}), f32[2048,512]{1,0:T(8,128)}) %all-reduce.21.cloned.1.call-update) | async-done | bytes 4194320 | tf_op jit(solution)/shard_map/psum | solution.py:303
  677.1 26.2 %all-gather.7 = f32[8,2,256]{2,1,0:T(2,128)S(1)} all-gather(f32[1,2,256]{2,1,0:T(2,128)S(1)} %bitcast.837), channel_id=5, replica_groups=mesh['seq'=8,'head'=4] {'seq'}, dimensions={0}, use_global_device_ids=true | all-gather | bytes 18432 | tf_op jit(solution)/shard_map/all_gather | solution.py:23
  704.6 8.9 while.77
  721.1 348.3 %while.78 = (s32[]{:T(128)}, f32[2,256,64]{1,2,0:T(8,128)S(1)}, f32[2,256]{1,0:T(2,128)S(1)}, f32[4,512,2,256]{1,0,3,2:T(4,128)}, f32[4,512,2,256]{3,1,2,0:T(8,1...) while((s32[]{:T(128)}, f32[2,256,64]{1,2,0:T(8,128)S(1)}, ...), condition=%wide.region_45.46_spmd, body=%wide.region_31.45_spmd.sunk | while | flops 6676042752 | bytes 89419472 | solution.py:157
  782.3 21.0 %dynamic_update_slice.74 = f32[4,512,2,256]{1,0,3,2:T(4,128)} dynamic-update-slice(f32[4,512,2,256]{1,0,3,2:T(4,128)} %get-tuple-element.1627, f32[1,512,2,256]{1,0,3,2:T(1,128)S(1)} %copy.453, s32[]{:T(128)S(6)} %sub.438, s32[]{:T(128)} %constant.327.clone.1..sunk.2, s32[]{:T(128)} %constant.327.clone.1..sunk.2, s32[]{:T(128)} %constant.327.clone.1..sunk.2) | dynamic-update-slice | bytes 2097156 | tf_op jit(solution)/shard_map/transpose(jvp())/while/body/jit(dynamic_update_index_in_dim)/dynamic_update_slice | solution.py:157
  869.2 21.0 %dynamic_update_slice.74 = f32[4,512,2,256]{1,0,3,2:T(4,128)} dynamic-update-slice(f32[4,512,2,256]{1,0,3,2:T(4,128)} %get-tuple-element.1627, f32[1,512,2,256]{1,0,3,2:T(1,128)S(1)} %copy.453, s32[]{:T(128)S(6)} %sub.438, s32[]{:T(128)} %constant.327.clone.1..sunk.2, s32[]{:T(128)} %constant.327.clone.1..sunk.2, s32[]{:T(128)} %constant.327.clone.1..sunk.2) | dynamic-update-slice | bytes 2097156 | tf_op jit(solution)/shard_map/transpose(jvp())/while/body/jit(dynamic_update_index_in_dim)/dynamic_update_slice | solution.py:157
  956.1 21.0 %dynamic_update_slice.74 = f32[4,512,2,256]{1,0,3,2:T(4,128)} dynamic-update-slice(f32[4,512,2,256]{1,0,3,2:T(4,128)} %get-tuple-element.1627, f32[1,512,2,256]{1,0,3,2:T(1,128)S(1)} %copy.453, s32[]{:T(128)S(6)} %sub.438, s32[]{:T(128)} %constant.327.clone.1..sunk.2, s32[]{:T(128)} %constant.327.clone.1..sunk.2, s32[]{:T(128)} %constant.327.clone.1..sunk.2) | dynamic-update-slice | bytes 2097156 | tf_op jit(solution)/shard_map/transpose(jvp())/while/body/jit(dynamic_update_index_in_dim)/dynamic_update_slice | solution.py:157
  1043.1 21.0 %dynamic_update_slice.74 = f32[4,512,2,256]{1,0,3,2:T(4,128)} dynamic-update-slice(f32[4,512,2,256]{1,0,3,2:T(4,128)} %get-tuple-element.1627, f32[1,512,2,256]{1,0,3,2:T(1,128)S(1)} %copy.453, s32[]{:T(128)S(6)} %sub.438, s32[]{:T(128)} %constant.327.clone.1..sunk.2, s32[]{:T(128)} %constant.327.clone.1..sunk.2, s32[]{:T(128)} %constant.327.clone.1..sunk.2) | dynamic-update-slice | bytes 2097156 | tf_op jit(solution)/shard_map/transpose(jvp())/while/body/jit(dynamic_update_index_in_dim)/dynamic_update_slice | solution.py:157
  1116.7 11.7 fusion.158
  1131.2 11.6 fusion.155
  1160.8 17.4 %all-reduce.13 = (bf16[512]{0:T(512)(128)(2,1)S(1)}, bf16[512]{0:T(512)(128)(2,1)S(1)}) all-reduce(bf16[512]{0:T(512)(128)(2,1)S(1)} %copy-done.107, bf16[512]{0:T(512)(128)(2,1)S(1)} %copy-done.108), channel_id=15, replica_groups=mesh['seq'=8,'head'=4] {'seq'}, use_global_device_ids=true, to_apply=%region_68.69.clone | all-reduce | flops 1024 | bytes 4096
  1184.6 41.6 %all-reduce.23.cloned.1.call-done = bf16[2048,512]{1,0:T(8,128)(2,1)} async-done(((bf16[2048,512]{1,0:T(8,128)(2,1)}), bf16[2048,512]{1,0:T(8,128)(2,1)}) %all-reduce.23.cloned.1.call-update) | async-done | bytes 2097168 | tf_op jit(solution)/shard_map/psum | solution.py:350
  1232.6 21.7 %all-reduce.12 = (f32[512]{0:T(512)S(1)}, f32[512]{0:T(512)S(1)}, f32[8,2]{1,0:T(8,128)S(1)}) all-reduce(f32[512]{0:T(512)S(1)} %get-tuple-element.941, f32[512]{0:T(512)S(1)} %get-tuple-element.950, f32[8,2]{1,0:T(8,128)S(1)} %broadcast_in_dim.176), channel_id=7, replica_groups=mesh['seq'=8,'head'=4] {'seq'}, use_global_device_ids=true, to_apply=%region_57.58.clone | all-reduce | flops 1040 | bytes 8320
  1259.7 31.8 %reduce-scatter.19.cloned.1.call-done = f32[128,64]{0,1:T(8,128)} async-done(((f32[128,512]{0,1:T(8,128)}), f32[128,64]{0,1:T(8,128)}) %reduce-scatter.19.cloned.1.call-update) | async-done | bytes 32784 | tf_op jit(solution)/shard_map/reduce_scatter | solution.py:365
  1291.4 64.1 %reduce-scatter.13.cloned.1.call-done = f32[64,128]{1,0:T(8,128)} async-done(((f32[512,128]{1,0:T(8,128)}), f32[64,128]{1,0:T(8,128)}) %reduce-scatter.13.cloned.1.call-update) | async-done | bytes 32784 | tf_op jit(solution)/shard_map/reduce_scatter | solution.py:361
  1355.6 64.0 %reduce-scatter.15.cloned.1.call-done = f32[64,128]{1,0:T(8,128)} async-done(((f32[512,128]{1,0:T(8,128)}), f32[64,128]{1,0:T(8,128)}) %reduce-scatter.15.cloned.1.call-update) | async-done | bytes 32784 | tf_op jit(solution)/shard_map/reduce_scatter | solution.py:362
  1419.6 64.0 %reduce-scatter.17.cloned.1.call-done = f32[64,128]{1,0:T(8,128)} async-done(((f32[512,128]{1,0:T(8,128)}), f32[64,128]{1,0:T(8,128)}) %reduce-scatter.17.cloned.1.call-update) | async-done | bytes 32784 | tf_op jit(solution)/shard_map/reduce_scatter | solution.py:363
  (966 shorter events, 611.0 us)
Async XLA Ops:
  7.2 145.4 %all-gather.13.cloned.1.call-start = ((), (), s32[]{:S(2)}) async-start(), calls=%async_computation.8 | async-start | bytes 2621440 | tf_op jit(solution)/shard_map/all_gather | solution.py:221
  7.9 397.8 %all-gather.17.cloned.1.call-start = ((), (), s32[]{:S(2)}) async-start(), calls=%async_computation.20 | async-start | bytes 1179648 | tf_op jit(solution)/shard_map/all_gather | solution.py:23
  37.4 121.6 %copy-start.101 = (f32[512]{0:T(512)}, f32[512]{0:T(512)S(1)}, u32[]{:S(2)}) copy-start(f32[512]{0:T(512)S(1)} %convert_element_type.281) | copy-start | bytes 6148
  53.9 168.7 %copy-start.103 = (bf16[512,2]{0,1:T(2,128)(2,1)}, bf16[512,2]{0,1:T(2,128)(2,1)S(1)}, u32[]{:S(2)}) copy-start(bf16[512,2]{0,1:T(2,128)(2,1)S(1)} %reshape.709) | copy-start | bytes 6148
  86.8 72.2 %copy-start.56 = (bf16[512,128]{1,0:T(8,128)(2,1)}, bf16[512,128]{1,0:T(8,128)(2,1)S(1)}, u32[]{:S(2)}) copy-start(bf16[512,128]{1,0:T(8,128)(2,1)S(1)} %all_gather.71) | copy-start | bytes 393220
  151.9 206.2 %copy-start.86 = (f32[2048]{0:T(1024)}, f32[2048]{0:T(1024)S(1)}, u32[]{:S(2)}) copy-start(f32[2048]{0:T(1024)S(1)} %convert_select_fusion) | copy-start | bytes 24580
  223.3 134.9 %copy-start.85 = (f32[2048,2]{0,1:T(2,128)}, f32[2048,2]{0,1:T(2,128)S(1)}, u32[]{:S(2)}) copy-start(f32[2048,2]{0,1:T(2,128)S(1)} %get-tuple-element.1109) | copy-start | bytes 49156
  223.3 103.0 %copy-start.105 = (bf16[128,64]{0,1:T(8,128)(2,1)S(1)}, bf16[128,64]{0,1:T(8,128)(2,1)}, u32[]{:S(2)}) copy-start(bf16[128,64]{0,1:T(8,128)(2,1)} %param.36) | copy-start | bytes 49156
  325.2 80.6 %copy-start.91 = (s32[4,512]{1,0:T(4,128)}, s32[4,512]{1,0:T(4,128)S(1)}, u32[]{:S(2)}) copy-start(s32[4,512]{1,0:T(4,128)S(1)} %get-tuple-element.1726) | copy-start | bytes 24580
  325.2 378.1 %copy-start.74 = (f32[4,512]{1,0:T(4,128)}, f32[4,512]{1,0:T(4,128)S(1)}, u32[]{:S(2)}) copy-start(f32[4,512]{1,0:T(4,128)S(1)} %get-tuple-element.1723) | copy-start | bytes 24580
  325.8 183.4 %all-reduce.19.cloned.1.call-start = ((), (), s32[]{:S(2)}) async-start(), calls=%async_computation.9 | async-start | bytes 8388608 | tf_op jit(solution)/shard_map/psum | solution.py:284
  357.9 292.0 %copy-start.89 = (f32[2048]{0:T(1024)}, f32[2048]{0:T(1024)S(1)}, u32[]{:S(2)}) copy-start(f32[2048]{0:T(1024)S(1)} %fusion.206) | copy-start | bytes 24580
  358.1 312.5 %copy-start.70 = (f32[2048]{0:T(1024)}, f32[2048]{0:T(1024)S(1)}, u32[]{:S(2)}) copy-start(f32[2048]{0:T(1024)S(1)} %convert_bitcast_fusion.2) | copy-start | bytes 24580
  359.5 311.2 %copy-start.64 = (f32[1,2,16,128]{3,2,1,0:T(8,128)}, f32[1,2,16,128]{3,2,1,0:T(8,128)S(1)}, u32[]{:S(2)}) copy-start(f32[1,2,16,128]{3,2,1,0:T(8,128)S(1)} %exponential_bitcast_fusion) | copy-start | bytes 49156
  359.5 290.5 %copy-start.79 = (f32[2048,2]{0,1:T(2,128)}, f32[2048,2]{0,1:T(2,128)S(1)}, u32[]{:S(2)}) copy-start(f32[2048,2]{0,1:T(2,128)S(1)} %fusion.193) | copy-start | bytes 49156
  405.8 308.5 %copy-start.87 = (f32[2,256]{1,0:T(2,128)}, f32[2,256]{1,0:T(2,128)S(1)}, u32[]{:S(2)}) copy-start(f32[2,256]{1,0:T(2,128)S(1)} %get-tuple-element.651) | copy-start | bytes 6148
  410.7 292.6 %copy-start.65 = (f32[2048,2]{0,1:T(2,128)}, f32[2048,2]{0,1:T(2,128)S(1)}, u32[]{:S(2)}) copy-start(f32[2048,2]{0,1:T(2,128)S(1)} %get-tuple-element.1065) | copy-start | bytes 49156
  415.6 93.6 %copy-start.10 = (bf16[2048,512]{1,0:T(8,128)(2,1)S(1)}, bf16[2048,512]{1,0:T(8,128)(2,1)}, u32[]{:S(2)}) copy-start(bf16[2048,512]{1,0:T(8,128)(2,1)} %all-gather.13.cloned.1.call-done) | copy-start | bytes 6291460
  418.4 115.2 %all-gather.15.cloned.1.call-start = ((), (), s32[]{:S(2)}) async-start(), calls=%async_computation.11 | async-start | bytes 2621440 | tf_op jit(solution)/shard_map/all_gather | solution.py:222
  418.9 218.3 %all-reduce.21.cloned.1.call-start = ((), (), s32[]{:S(2)}) async-start(), calls=%async_computation.12 | async-start | bytes 8388608 | tf_op jit(solution)/shard_map/psum | solution.py:303
  551.6 153.0 %all-gather.19.cloned.1.call-start = ((), (), s32[]{:S(2)}) async-start(), calls=%async_computation.21 | async-start | bytes 1179648 | tf_op jit(solution)/shard_map/all_gather | solution.py:23
  656.2 501.6 %reduce-scatter.21.cloned.1.call-start = ((), (), s32[]{:S(2)}) async-start(), calls=%async_computation.18 | async-start | bytes 589824 | tf_op jit(solution)/shard_map/reduce_scatter | solution.py:371
  660.8 498.5 %reduce-scatter.23.cloned.1.call-start = ((), (), s32[]{:S(2)}) async-start(), calls=%async_computation.19 | async-start | bytes 589824 | tf_op jit(solution)/shard_map/reduce_scatter | solution.py:374
  669.2 511.7 %reduce-scatter.25.cloned.1.call-start = ((), (), s32[]{:S(2)}) async-start(), calls=%async_computation.22 | async-start | bytes 294912
  1081.7 100.6 %reduce-scatter.11.cloned.1.call-start = ((), (), s32[]{:S(2)}) async-start(), calls=%async_computation.10 | async-start | bytes 2621440 | tf_op jit(solution)/shard_map/reduce_scatter | solution.py:291
  1086.0 140.2 %all-reduce.23.cloned.1.call-start = ((), (), s32[]{:S(2)}) async-start(), calls=%async_computation.13 | async-start | bytes 4194304 | tf_op jit(solution)/shard_map/psum | solution.py:350
  1148.2 143.2 %reduce-scatter.19.cloned.1.call-start = ((), (), s32[]{:S(2)}) async-start(), calls=%async_computation.17 | async-start | bytes 294912 | tf_op jit(solution)/shard_map/reduce_scatter | solution.py:365
  1152.7 202.9 %reduce-scatter.13.cloned.1.call-start = ((), (), s32[]{:S(2)}) async-start(), calls=%async_computation.14 | async-start | bytes 294912 | tf_op jit(solution)/shard_map/reduce_scatter | solution.py:361
  1154.3 72.0 %copy-start.96 = (f32[2048]{0:T(1024)S(1)}, f32[2048]{0:T(1024)}, u32[]{:S(2)}) copy-start(f32[2048]{0:T(1024)} %copy-done.95) | copy-start | bytes 24580
  1154.3 72.0 %copy-start.102 = (f32[512]{0:T(512)S(1)}, f32[512]{0:T(512)}, u32[]{:S(2)}) copy-start(f32[512]{0:T(512)} %copy-done.101) | copy-start | bytes 6148
  1154.3 265.3 %reduce-scatter.15.cloned.1.call-start = ((), (), s32[]{:S(2)}) async-start(), calls=%async_computation.15 | async-start | bytes 294912 | tf_op jit(solution)/shard_map/reduce_scatter | solution.py:362
  1157.1 326.5 %reduce-scatter.17.cloned.1.call-start = ((), (), s32[]{:S(2)}) async-start(), calls=%async_computation.16 | async-start | bytes 294912 | tf_op jit(solution)/shard_map/reduce_scatter | solution.py:363
  (165 other events, 1843.6 us)
Sparse Core Ops, SparseCore 0:
  9.6 25.2 all-gather.12
  326.0 39.0 all-gather.16
  418.5 90.7 all-reduce.18
  510.8 22.7 all-gather.14
  551.7 85.4 all-reduce.20
  656.4 40.3 all-gather.18
  700.1 60.8 reduce-scatter.20
  764.7 60.8 reduce-scatter.22
  1081.8 57.6 reduce-scatter.24
  1141.9 30.4 reduce-scatter.10
  1174.9 51.3 all-reduce.22
  1230.0 61.3 reduce-scatter.18
  1295.3 60.2 reduce-scatter.12
  1359.3 60.2 reduce-scatter.14
  1423.3 60.2 reduce-scatter.16
where the time goes:
time: 1500 us; the launch traced here: 1490 us
  waiting for transfers between devices  387 us (26%)
  blocking collectives  345 us (23%)
  local copies, waits for them, and re-layouts  312 us (21%)
  matrix products  288 us (19%)
  other arithmetic  138 us (9%)
  between operations  18 us (1%)
    dynamic_update_slice x28, local copies, waits for them, and re-layouts, attention_part(): lax.scan(jax.checkpoint(block_step), start, xs)  128 us
    psum x1, waiting for transfers between devices, shards(): lax.psum(jnp.dot(grad_hidden, full_up.T, preferred_element_type=jnp.float...  85.6 us
    all_gather x3, blocking collectives, carried_in(): gathered = jax.tree.map(lambda a: lax.all_gather(a, axis), part)  70.1 us
    dot_general x16, matrix products, block_step(): jnp.einsum('ihm,shm->ish', query_feat, key_feat, precision=highest)  65.4 us
    reduce_scatter x1, waiting for transfers between devices, shards(): lax.psum_scatter(grad_query_w, 'seq', scatter_dimension=0, tiled=True)  64.1 us
    reduce_scatter x1, waiting for transfers between devices, shards(): lax.psum_scatter(grad_key_w, 'seq', scatter_dimension=0, tiled=True)  64 us
    reduce_scatter x1, waiting for transfers between devices, shards(): lax.psum_scatter(grad_value_w, 'seq', scatter_dimension=0, tiled=True)  64 us
    unnamed x3, blocking collectives  62.2 us
  transfers between devices with their start and end apart: 15, of which 8 were waited for; matrix products, arithmetic and copies ran while one was open for 34% of the time, Pallas kernels for 0%

commit v1 on v0

v1 whole, which is shorter than its diff:
```python
import functools
import math

import jax
import jax.numpy as jnp
from jax import lax
from jax.experimental import pallas as pl
from jax.experimental.pallas import tpu as pltpu
from jax.sharding import PartitionSpec as P

BF, F32, I32 = jnp.bfloat16, jnp.float32, jnp.int32
MESH = pl.DeviceIdType.MESH
HEADS, HEAD_DIM, FEATS = 8, 64, 128
PAIRS = HEADS // 2
LANES = 128
EPS, FLOOR2, GATE_PEN = 1e-5, 0.0625, 0.5
TABLE_SCALE = 1.0 / math.sqrt(21845.0)
FEAT_SCALE = 1.0 / math.sqrt(FEATS)
INV_TWO_PI, TWO_PI = 1.0 / (2.0 * math.pi), 2.0 * math.pi
SIN = (0.9999996027571254, -0.16666553170295112, 0.008332405799301931, -0.00019808693226998236,
       2.6997700314773084e-06, -2.036409109746239e-08)
COS = (0.9999992193982472, -0.4999942543676011, 0.04165980908449851, -0.0013858873219640337,
       2.420384320646774e-05, -2.1976364824224383e-07)
ERFC = (0.254829592, -0.284496736, 1.421413741, -1.453152027, 1.061405429)
ATT = 4 * LANES
VMEM_BYTES = 56 * 1024 * 1024


def nn(a, b):
    return lax.dot_general(a, b, (((1,), (0,)), ((), ())), preferred_element_type=F32)


def nt(a, b):
    return lax.dot_general(a, b, (((1,), (1,)), ((), ())), preferred_element_type=F32)


def tn(a, b):
    return lax.dot_general(a, b, (((0,), (0,)), ((), ())), preferred_element_type=F32)


def halves(x, axis=1):
    hi = x.astype(BF)
    return jnp.concatenate([hi, (x - hi.astype(F32)).astype(BF)], axis=axis)


def iota(shape, dim):
    return lax.broadcasted_iota(I32, shape, dim)


def rows_loop(total, step, body):
    step = min(step, total)

    def one(i, carry):
        body(pl.ds(pl.multiple_of(i * step, step), step), i * step, step)
        return carry

    lax.fori_loop(0, total // step, one, 0)


def pair_loop(body):
    def one(p, carry):
        body(p)
        return carry

    lax.fori_loop(0, PAIRS, one, 0)


def head_ones(rows, cols, row_span, col_span):
    same = (iota((rows, cols), 0) // row_span) % 2 == iota((rows, cols), 1) // col_span
    return jnp.where(same, 1.0, 0.0).astype(BF)


def marks(pos, base, lengths_ref):
    start = jnp.int32(0)
    segment = jnp.zeros(pos.shape, I32)
    reset = jnp.zeros(pos.shape, F32)
    carry = jnp.ones(pos.shape, F32)
    for d in range(lengths_ref.shape[0]):
        segment = segment + jnp.where(pos >= start, 1, 0)
        reset = jnp.where(pos == start, 1.0, reset)
        carry = jnp.where((pos >= start) & (pos - start <= pos - base), 0.0, carry)
        start = start + lengths_ref[d]
    live = jnp.where(pos < start, 1.0, 0.0)
    segment = segment + jnp.where(pos >= start, 1, 0)
    return segment, reset, live, carry, start


def horner(coefs, t):
    acc = jnp.full_like(t, coefs[-1])
    for c in coefs[-2::-1]:
        acc = acc * t + c
    return acc


def sincos(angle):
    r = angle - jnp.round(angle * INV_TWO_PI) * TWO_PI
    t = r * r
    return r * horner([c * FEAT_SCALE for c in SIN], t), horner([c * FEAT_SCALE for c in COS], t)


def gelu_parts(x):
    t = 1.0 / (1.0 + (0.3275911 / math.sqrt(2.0)) * jnp.abs(x))
    e = jnp.exp(-0.5 * x * x)
    q = 0.5 * t * horner(ERFC, t) * e
    cdf = jnp.where(x < 0.0, q, 1.0 - q)
    return x * cdf, cdf + x * e * (1.0 / math.sqrt(2.0 * math.pi))


def norm_stats(x):
    center = jnp.mean(x, axis=-1, keepdims=True)
    spread = jnp.mean(x * x, axis=-1, keepdims=True) - center * center
    inv = lax.rsqrt(spread + EPS)
    return (x - center) * inv, inv


def norm_back(grad, xhat, inv, gain):
    p = grad * gain
    return inv * (p - jnp.mean(p, axis=-1, keepdims=True) - xhat * jnp.mean(p * xhat, axis=-1, keepdims=True))


def by_eight(x):
    return jnp.sum(x.reshape(x.shape[0] // 8, 8, x.shape[1]), axis=0)


def panel(ref, p, cols):
    x = ref[p, :, :, :, cols]
    return x.reshape(x.shape[0] * x.shape[1] * x.shape[2], x.shape[3])


def low_lanes(rows):
    return iota((rows, LANES), 1) < HEAD_DIM


def widen(pair, a):
    return pair[:, a * HEAD_DIM : a * HEAD_DIM + 1]


def head_values(v, a, low):
    one = jnp.ones_like(v)
    return jnp.where(low, v, one) if a == 0 else jnp.where(low, one, v)


def state_of(mem, nrm, p, a):
    own = mem[p, a * HEAD_DIM : (a + 1) * HEAD_DIM, :]
    rest = jnp.broadcast_to(nrm[pl.ds(2 * p + a, 1), :], own.shape).astype(BF)
    return jnp.concatenate([own, rest] if a == 0 else [rest, own], axis=0)


def front(T, base, r):
    D = r.tok.shape[1]
    pick = jnp.where(iota((16, LANES), 0) == iota((16, LANES), 1), 1.0, 0.0).astype(BF)
    for p in range(PAIRS):
        rows = nt(pick, panel(r.ga, p, slice(3 * LANES, 4 * LANES)))
        r.gate[2 * p : 2 * p + 2, :] = rows[0:2]
        r.gate[8 + 2 * p : 10 + 2 * p, :] = rows[0:2]
        r.bias[2 * p : 2 * p + 1, :] = rows[6:7] + rows[7:8] + rows[8:9]
        r.bias[2 * p + 1 : 2 * p + 2, :] = rows[9:10] + rows[10:11] + rows[11:12]
        if p == 0:
            r.vec[...] = rows[0:8]

    def norm_rows(rows, at, n):
        xhat, _ = norm_stats(r.tok[rows, :].astype(F32))
        r.normed[rows, :] = (xhat * r.vec[2:3, :] + r.vec[3:4, :]).astype(BF)

    rows_loop(T, 64, norm_rows)

    logits = nt(r.gate[...].astype(BF), r.normed[...])[0:8] + r.bias[:, 0:1]
    r.logits[...] = logits
    pos = base + iota((8, T), 1)
    seg_row, reset_row, live_row, carry_row, _ = marks(pos, base, r.lengths)
    decay = -(jnp.log1p(jnp.exp(-jnp.abs(logits))) + jnp.maximum(-logits, 0.0)) * live_row * (1.0 - reset_row)
    run = decay
    lane = iota((8, T), 1)
    shift = 1
    while shift < T:
        run = run + jnp.where(lane >= shift, pltpu.roll(run, shift, 1), 0.0)
        shift *= 2
    r.run[...] = run
    r.total[...] = jnp.broadcast_to(jnp.exp(run[:, T - 1 : T]) * carry_row[:, T - 1 : T], (8, LANES))
    hi = run.astype(BF).astype(F32)
    mid = (run - hi).astype(BF).astype(F32)
    low3 = run - hi - mid
    run3 = jnp.concatenate([hi, mid, low3, jnp.zeros_like(hi)], axis=0).astype(BF)

    def mask_rows(rows, at, n):
        row_pos = base + at + iota((n, 1), 0)
        seg_col = marks(row_pos, base, r.lengths)[0]
        seg1, live1, pos1 = seg_row[0:1], live_row[0:1], pos[0:1]
        allowed = (seg_col == seg1) & (pos1 <= row_pos) & (live1 > 0.0)
        r.mask[rows, :] = jnp.where(allowed, 0.0, -1e30)

    rows_loop(T, 64, mask_rows)

    hash_seed = r.seed[0] * jnp.int32(-2048144789)
    ones2 = head_ones(2 * LANES, 2 * LANES, HEAD_DIM, LANES)
    low = low_lanes(T)
    last_seg = marks(base + T - 1 + iota((8, LANES), 1) * 0, base, r.lengths)[0][0:1, 0:1]
    col_pos = base + iota((T, LANES), 0)
    seg_col, _, live_col, _, _ = marks(col_pos, base, r.lengths)
    end_live = jnp.where(seg_col == last_seg, live_col, 0.0)

    def features(p, u, out):
        r.s1[...] = nn(jnp.concatenate([u, u], axis=1), r.tab[p])
        uf = u.astype(F32)
        r.s2[...] = nn(halves(uf * uf), ones2)

        def body(rows, at, n):
            s, c = sincos(r.s1[rows, :] * (lax.rsqrt(r.s2[rows, :] + 1e-6) * TABLE_SCALE))
            for a in range(2):
                out[2 * p + a, rows, 0:FEATS] = s[:, a * FEATS : (a + 1) * FEATS].astype(BF)
                out[2 * p + a, rows, FEATS : 2 * FEATS] = c[:, a * FEATS : (a + 1) * FEATS].astype(BF)

        rows_loop(T, 64, body)

    def first(p):
        place = (p * LANES + iota((LANES, LANES), 0)) * FEATS + iota((LANES, LANES), 1)
        y = place * jnp.int32(-1640531535) + hash_seed
        y = y ^ lax.shift_right_logical(y, jnp.int32(15))
        y = y * jnp.int32(739982445)
        y = y ^ lax.shift_right_logical(y, jnp.int32(13))
        y = y * jnp.int32(695872825)
        y = y ^ lax.shift_right_logical(y, jnp.int32(16))
        s = jnp.full(y.shape, -510, I32)
        for k in range(4):
            s = s + (lax.shift_right_logical(y, jnp.int32(8 * k)) & jnp.int32(255))
        top = iota((LANES, LANES), 0) < HEAD_DIM
        odd = s & 1

        def diagonal(x):
            x = x.astype(F32)
            return jnp.concatenate([jnp.where(top, x, 0.0), jnp.where(top, 0.0, x)], axis=1).astype(BF)

        r.tab[p, 0:LANES, :] = diagonal(s - odd)
        r.tab[p, LANES:, :] = diagonal(odd)
        r.tabn[p] = diagonal(s)
        qkv = nn(r.normed[...], panel(r.ga, p, slice(0, 3 * LANES))).astype(BF)
        r.q[p] = qkv[:, 0:LANES]
        r.k[p] = qkv[:, LANES : 2 * LANES]
        r.v[p] = qkv[:, 2 * LANES :]
        chosen = iota((32, LANES), 0) % 8 == 2 * p + iota((32, LANES), 1) // HEAD_DIM
        r.rb[p] = tn(run3, jnp.where(chosen, 1.0, 0.0).astype(BF))

        features(p, r.k[p], r.kf)
        decay_end = jnp.exp(r.rb[p, T - 1 : T, :] - r.rb[p]) * end_live
        v = r.v[p].astype(F32)
        for a in range(2):
            scaled = (head_values(v, a, low) * widen(decay_end, a)).astype(BF)
            state = tn(scaled, r.kf[2 * p + a])
            r.mem[p, a * HEAD_DIM : (a + 1) * HEAD_DIM, :] = state[a * HEAD_DIM : (a + 1) * HEAD_DIM].astype(BF)
            at = HEAD_DIM if a == 0 else 0
            r.nrm32[pl.ds(2 * p + a, 1), :] = state[at : at + 1]

    r.nrm32[...] = jnp.zeros_like(r.nrm32)
    pair_loop(first)
    r.nrm[...] = r.nrm32[...].astype(BF)

    def second(p):
        features(p, r.q[p], r.qf)
        v = r.v[p]
        for a in range(2):
            h = 2 * p + a
            r.s[...] = nt(r.qf[h], r.kf[h])
            run_row = r.run[pl.ds(h, 1), :]

            def body(rows, at, n):
                gap = jnp.minimum(widen(r.rb[p, rows, :], a) - run_row, r.mask[rows, :])
                r.w[h, rows, :] = (r.s[rows, :] * jnp.exp(gap)).astype(BF)

            rows_loop(T, 64, body)
            r.own[h] = nn(r.w[h], head_values(v, a, low))

    pair_loop(second)


def middle(T, base, r):
    D = r.tok.shape[1]
    low = low_lanes(T)
    col_pos = base + iota((T, LANES), 0)
    _, _, live_col, carry_col, _ = marks(col_pos, base, r.lengths)
    r.nin32[...] = r.nin[...].astype(F32)

    def join(p):
        factor = jnp.exp(r.rb[p]) * carry_col
        total = []
        for a in range(2):
            h = 2 * p + a
            carried = nt(r.qf[h], state_of(r.min, r.nin32, p, a))
            joined = r.own[h] + widen(factor, a) * carried
            r.joined[h] = joined
            total.append(joined)
        num = jnp.where(low, total[0], total[1])
        z = pltpu.roll(jnp.where(low, total[1], total[0]), HEAD_DIM, 1)
        r.num[p] = num
        r.z[p] = z
        r.att[p] = (live_col * num * lax.rsqrt(z * z + FLOOR2)).astype(BF)

    pair_loop(join)
    o = slice(0, LANES)
    branch = None
    for p in range(0, PAIRS, 2):
        part = nt(
            jnp.concatenate([r.att[p], r.att[p + 1]], axis=1),
            jnp.concatenate([panel(r.gf, p, o), panel(r.gf, p + 1, o)], axis=1),
        )
        branch = part if branch is None else branch + part
    r.mid[...] = branch

    def norm_rows(rows, at, n):
        mid = r.mid[rows, :] + r.tok[rows, :].astype(F32)
        r.mid[rows, :] = mid
        xhat, inv = norm_stats(mid)
        r.xhat[rows, :] = xhat
        r.inv[rows, :] = jnp.broadcast_to(inv, (n, LANES))
        r.two[rows, :] = (xhat * r.vec[4:5, :] + r.vec[5:6, :]).astype(BF)

    rows_loop(T, 64, norm_rows)
    r.acc1[...] = jnp.zeros_like(r.acc1)
    r.acc2[...] = jnp.zeros_like(r.acc2)
    ff = (r.gf.shape[-1] - LANES) // 2
    u, d = slice(LANES, LANES + ff), slice(LANES + ff, LANES + 2 * ff)

    def feed(p):
        up, down = panel(r.gf, p, u), panel(r.gf, p, d)
        r.h1[...] = nn(r.two[...], up)
        r.h2[...] = nn(r.cot[...], down)

        def body(rows, at, n):
            value, slope = gelu_parts(r.h1[rows, :])
            r.act[rows, :] = value.astype(BF)
            r.gh[rows, :] = (r.h2[rows, :] * slope).astype(BF)

        rows_loop(T, 64, body)
        r.acc1[...] += nt(r.act[...], down)
        r.acc2[...] += nt(r.gh[...], up)
        put_panel(r.ggf, p, u, tn(r.two[...], r.gh[...]))
        put_panel(r.ggf, p, d, tn(r.cot[...], r.act[...]))

    pair_loop(feed)
    r.sums[...] = jnp.zeros_like(r.sums)

    def finish(rows, at, n):
        r.result[rows, :] = (r.mid[rows, :] + r.acc1[rows, :]).astype(BF)
        xhat, gn = r.xhat[rows, :], r.acc2[rows, :]
        r.sums[0:8, :] += by_eight(gn * xhat)
        r.sums[8:16, :] += by_eight(gn)
        back = norm_back(gn, xhat, r.inv[rows, 0:1], r.vec[4:5, :])
        grad = r.cot[rows, :].astype(F32) + back
        r.gmid[rows, :] = grad
        r.gb[rows, :] = grad.astype(BF)

    rows_loop(T, 64, finish)
    r.fsum[0:1, :] = jnp.sum(r.sums[0:8, :], axis=0, keepdims=True)
    r.fsum[1:2, :] = jnp.sum(r.sums[8:16, :], axis=0, keepdims=True)
    ones1 = head_ones(2 * LANES, LANES, HEAD_DIM, HEAD_DIM)
    row_ones = jnp.ones((16, 2 * LANES), BF)
    first_half = iota((T, LANES), 1) % HEAD_DIM < HEAD_DIM // 2
    r.bn32[...] = jnp.zeros_like(r.bn32)

    def back(p):
        put_panel(r.ggf, p, o, tn(r.gb[...], r.att[p]))
        g = nn(r.gb[...], panel(r.gf, p, o)).astype(BF).astype(F32) * live_col
        num, z = r.num[p], r.z[p]
        rden = lax.rsqrt(z * z + FLOOR2)
        dn = (g * rden).astype(BF).astype(F32)
        dz = nn(halves(dn * num), ones1) * (z * rden * rden)
        dz = pltpu.roll(dz * (-2.0 / HEAD_DIM), HEAD_DIM, 1)
        rough = dz.astype(BF).astype(F32)
        dz = jnp.where(first_half, rough, dz - rough)
        factor = jnp.exp(r.rb[p]) * carry_col
        for a in range(2):
            h = 2 * p + a
            joint = (jnp.where(low, dn, dz) if a == 0 else jnp.where(low, dz, dn)).astype(BF)
            r.dn[h] = joint
            r.dr[pl.ds(h, 1), :] = nt(row_ones, halves(joint.astype(F32) * r.joined[h]))[0:1]
            adj = tn(joint, (r.qf[h].astype(F32) * widen(factor, a)).astype(BF))
            r.adj[p, a * HEAD_DIM : (a + 1) * HEAD_DIM, :] = adj[a * HEAD_DIM : (a + 1) * HEAD_DIM].astype(BF)
            at, half = (1 - a) * HEAD_DIM, HEAD_DIM // 2
            r.bn32[pl.ds(h, 1), :] = 0.5 * (adj[at : at + 1] + adj[at + half : at + half + 1])

    pair_loop(back)
    r.bn[...] = r.bn32[...].astype(BF)


def put_panel(ref, p, cols, x):
    shape = ref.shape[1:4] + (x.shape[1],)
    ref[p, :, :, :, cols] = x.astype(BF).reshape(shape)


def back(T, base, r, tokens_all):
    D = r.tok.shape[1]
    low = low_lanes(T)
    col_pos = base + iota((T, LANES), 0)
    seg_col, _, live_col, carry_col, _ = marks(col_pos, base, r.lengths)
    last_seg = marks(base + T - 1 + iota((8, LANES), 1) * 0, base, r.lengths)[0][0:1, 0:1]
    end_live = jnp.where(seg_col == last_seg, live_col, 0.0)
    r.nin32[...] = r.nin[...].astype(F32)
    r.bend32[...] = r.bend[...].astype(F32)
    ones1 = head_ones(2 * LANES, LANES, HEAD_DIM, HEAD_DIM)
    row_ones = jnp.ones((16, 2 * LANES), BF)
    r.acc1[...] = jnp.zeros_like(r.acc1)

    def feature_back(p, u, da):
        ds = nt(da, r.tabn[p]) * TABLE_SCALE
        uf = u.astype(F32)
        inv = lax.rsqrt(nn(halves(uf * uf), ones1) + 1e-6)
        uh = uf * inv
        return (inv * (ds - uh * nn(halves(uh * ds), ones1))).astype(BF)

    def pair(p):
        v, vf = r.v[p], None
        factor = jnp.exp(r.rb[p]) * carry_col
        decay_end = jnp.exp(r.rb[p, T - 1 : T, :] - r.rb[p]) * end_live
        grad_v = []
        for a in range(2):
            h = 2 * p + a
            r.s[...] = nt(r.dn[h], head_values(v, a, low))
            run_row = r.run[pl.ds(h, 1), :]

            def body(rows, at, n):
                gap = jnp.minimum(widen(r.rb[p, rows, :], a) - run_row, r.mask[rows, :])
                r.ds[rows, :] = (r.s[rows, :] * jnp.exp(gap)).astype(BF)

            rows_loop(T, 64, body)
            end = state_of(r.aend, r.bend32, p, a)
            kf, qf = r.kf[h], r.qf[h]
            hv = head_values(v, a, low)
            r.s1[...] = nn(r.ds[...], kf) + widen(factor, a) * nn(r.dn[h], state_of(r.min, r.nin32, p, a))
            r.s2[...] = tn(r.ds[...], qf) + widen(decay_end, a) * nn(hv, end)
            late = widen(decay_end, a) * nt(kf, end)
            grad_hv = tn(r.w[h], r.dn[h]) + late
            grad_v.append(grad_hv)
            lanes = slice(a * FEATS, (a + 1) * FEATS)

            def angles(rows, at, n):
                for source, feat, to in ((r.s1, r.qf, r.daq), (r.s2, r.kf, r.dak)):
                    x = source[rows, :]
                    f = feat[h, rows, :].astype(F32)
                    to[rows, lanes] = (x[:, :FEATS] * f[:, FEATS:] - x[:, FEATS:] * f[:, :FEATS]).astype(BF)

            rows_loop(T, 64, angles)
            hvf = hv.astype(F32)
            k_side = nt(row_ones, halves(hvf * grad_hv))
            r.drun[pl.ds(h, 1), :] = r.dr[pl.ds(h, 1), :] - k_side[0:1]
            own = slice(a * HEAD_DIM, (a + 1) * HEAD_DIM)
            owed = jnp.sum(r.aend[p, own, :].astype(F32) * r.min[p, own, :].astype(F32), axis=0, keepdims=True)
            owed = owed + HEAD_DIM * r.bend32[pl.ds(h, 1), :] * r.nin32[pl.ds(h, 1), :]
            owed = r.total[pl.ds(h, 1), 0:1] * jnp.sum(owed, axis=1, keepdims=True)
            owed = owed + jnp.sum(jnp.sum(hvf * late, axis=0, keepdims=True), axis=1, keepdims=True)
            r.owed[pl.ds(h, 1), :] = jnp.broadcast_to(owed, (1, LANES))
        grads = jnp.concatenate(
            [
                feature_back(p, r.q[p], r.daq[...]),
                feature_back(p, r.k[p], r.dak[...]),
                jnp.where(low, grad_v[0], grad_v[1]).astype(BF),
            ],
            axis=1,
        )
        r.acc1[...] += nt(grads, panel(r.ga, p, slice(0, 3 * LANES)))
        put_panel(r.gga, p, slice(0, 3 * LANES), tn(r.normed[...], grads))

    pair_loop(pair)
    pos = base + iota((8, T), 1)
    _, reset_row, live_row, _, filled = marks(pos, base, r.lengths)
    lane = iota((8, T), 1)
    run = r.drun[...]
    shift = 1
    while shift < T:
        run = run + jnp.where(lane < T - shift, pltpu.roll(run, T - shift, 1), 0.0)
        shift *= 2
    grad_decay = run + r.owed[:, 0:1]
    logits = r.logits[...]
    e = jnp.exp(-jnp.abs(logits))
    small, large = e / (1.0 + e), 1.0 / (1.0 + e)
    gate = jnp.where(logits >= 0.0, large, small)
    rest = jnp.where(logits >= 0.0, small, large)
    penalty = GATE_PEN * tokens_all / HEADS / jnp.broadcast_to(filled, (8, T)).astype(F32)
    grad_logits = grad_decay * live_row * (1.0 - reset_row) * rest + penalty * live_row * gate * rest
    both = halves(grad_logits, 0)
    r.acc1[...] += tn(both, r.gate[...].astype(BF))
    gate_rows = nn(both, r.normed[...])
    gate_rows = gate_rows[0:8] + gate_rows[8:16]
    bias = jnp.broadcast_to(jnp.sum(grad_logits, axis=1, keepdims=True), (8, D))
    r.sums[...] = jnp.zeros_like(r.sums)

    def finish(rows, at, n):
        xhat, inv = norm_stats(r.tok[rows, :].astype(F32))
        gn = r.acc1[rows, :]
        r.sums[0:8, :] += by_eight(gn * xhat)
        r.sums[8:16, :] += by_eight(gn)
        r.gtok[rows, :] = r.gmid[rows, :] + norm_back(gn, xhat, inv, r.vec[2:3, :])

    rows_loop(T, 64, finish)
    norm_gain = jnp.sum(r.sums[0:8, :], axis=0, keepdims=True)
    norm_shift = jnp.sum(r.sums[8:16, :], axis=0, keepdims=True)
    spread = jnp.where(iota((16, LANES), 0) == iota((16, LANES), 1), 1.0, 0.0).astype(BF)
    for p in range(PAIRS):
        pair_bias = bias[2 * p : 2 * p + 2]
        rough = pair_bias.astype(BF).astype(F32)
        rows = jnp.concatenate(
            [gate_rows[2 * p : 2 * p + 2], norm_gain, norm_shift, r.fsum[0:2, :], rough, pair_bias - rough, jnp.zeros((6, D), F32)],
            axis=0,
        )
        put_panel(r.gga, p, slice(3 * LANES, 4 * LANES), tn(rows.astype(BF), spread))


class Refs:
    def __init__(self, **refs):
        self.__dict__.update(refs)


def buffers(T, D, att, rest, ff, seq):
    z = (PAIRS, seq // 2, 2, D // seq)
    pair = (PAIRS, T, LANES)
    return {
        "ga": (z + (att,), BF), "gf": (z + (rest,), BF), "gga": (z + (att,), BF), "ggf": (z + (rest,), BF),
        "gate": ((16, D), F32), "bias": ((8, D), F32), "vec": ((8, D), F32), "normed": ((T, D), BF),
        "logits": ((8, T), F32), "run": ((8, T), F32), "total": ((8, LANES), F32), "mask": ((T, T), F32),
        "s1": ((T, 2 * FEATS), F32), "s2": ((T, 2 * FEATS), F32), "s": ((T, T), F32),
        "tab": ((PAIRS, 2 * LANES, 2 * FEATS), BF), "tabn": ((PAIRS, LANES, 2 * FEATS), BF),
        "q": (pair, BF), "k": (pair, BF), "v": (pair, BF), "rb": (pair, F32),
        "qf": ((HEADS, T, 2 * FEATS), BF), "kf": ((HEADS, T, 2 * FEATS), BF),
        "mem": ((PAIRS, LANES, 2 * FEATS), BF), "nrm": ((16, 2 * FEATS), BF), "nrm32": ((16, 2 * FEATS), F32),
        "min": ((PAIRS, LANES, 2 * FEATS), BF), "nin": ((16, 2 * FEATS), BF), "nin32": ((16, 2 * FEATS), F32),
        "adj": ((PAIRS, LANES, 2 * FEATS), BF), "bn": ((16, 2 * FEATS), BF), "bn32": ((16, 2 * FEATS), F32),
        "aend": ((PAIRS, LANES, 2 * FEATS), BF), "bend": ((16, 2 * FEATS), BF), "bend32": ((16, 2 * FEATS), F32),
        "w": ((HEADS, T, T), BF), "own": ((HEADS, T, LANES), F32), "joined": ((HEADS, T, LANES), F32), "num": (pair, F32), "z": (pair, F32),
        "att": (pair, BF), "mid": ((T, D), F32), "xhat": ((T, D), F32), "inv": ((T, LANES), F32), "two": ((T, D), BF),
        "acc1": ((T, D), F32), "acc2": ((T, D), F32), "h1": ((T, ff), F32), "h2": ((T, ff), F32),
        "act": ((T, ff), BF), "gh": ((T, ff), BF), "sums": ((16, D), F32), "fsum": ((8, D), F32),
        "result": ((T, D), BF), "gmid": ((T, D), F32), "gb": ((T, D), BF), "dr": ((8, T), F32), "dn": ((HEADS, T, LANES), BF),
        "ds": ((T, T), BF), "daq": ((T, 2 * FEATS), BF), "dak": ((T, 2 * FEATS), BF),
        "drun": ((8, T), F32), "owed": ((8, LANES), F32), "gtok": ((T, D), F32),
    }


FRONT = (
    ("ga",),
    ("gate", "vec", "normed", "logits", "run", "total", "mask", "tabn", "q", "k", "v", "rb", "qf", "kf", "mem", "nrm", "w", "own"),
    ("bias", "s1", "s2", "s", "tab", "nrm32"),
)
MIDDLE = (
    ("gf", "vec", "rb", "qf", "own", "min", "nin"),
    ("ggf", "result", "gmid", "fsum", "dr", "dn", "adj", "bn"),
    ("nin32", "joined", "num", "z", "att", "mid", "xhat", "inv", "two", "acc1", "acc2", "h1", "h2", "act", "gh", "sums", "gb", "bn32"),
)
BACK = (
    ("ga", "gate", "vec", "normed", "logits", "run", "total", "mask", "tabn", "q", "k", "v", "rb", "qf", "kf",
     "w", "min", "nin", "aend", "bend", "gmid", "fsum", "dr", "dn"),
    ("gga", "gtok"),
    ("nin32", "bend32", "s", "s1", "s2", "ds", "daq", "dak", "drun", "owed", "acc1", "sums"),
)


def here(T):
    return (lax.axis_index("seq") * lax.axis_size("head") + lax.axis_index("head")) * T


def stage(which, names, specs, outer, args, state):
    reads, writes, scratch = names
    shape = lambda n: jax.ShapeDtypeStruct(*specs[n])
    vmem, smem = pl.BlockSpec(memory_space=pltpu.VMEM), pl.BlockSpec(memory_space=pltpu.SMEM)

    def kernel(*refs):
        base_ref, lengths, seed, tok, cot = refs[:5]
        rest = dict(zip(reads + writes + scratch, refs[5:]))
        which(base_ref[0], Refs(lengths=lengths, seed=seed, tok=tok, cot=cot, **rest))

    out = pl.pallas_call(
        kernel,
        out_shape=[shape(n) for n in writes],
        in_specs=[smem] * 3 + [vmem] * (2 + len(reads)),
        out_specs=[vmem] * len(writes),
        scratch_shapes=[pltpu.VMEM(*specs[n]) for n in scratch],
        compiler_params=pltpu.CompilerParams(vmem_limit_bytes=VMEM_BYTES),
        name=outer,
    )(*args, *[state[n] for n in reads])
    state.update(zip(writes, out))


def scan_states(mem, nrm, total, reverse):
    seq, head = lax.axis_size("seq"), lax.axis_size("head")
    count = seq * head
    me = lax.axis_index("seq") * head + lax.axis_index("head")
    factor = total[:, 0]
    by_head = lambda x: jnp.repeat(x.reshape(PAIRS, 2), HEAD_DIM, axis=1)[:, :, None]
    state = (factor, mem.astype(F32), nrm[:HEADS].astype(F32))
    step = 1
    order = lambda pairs: [(b, a) for a, b in pairs] if reverse else pairs
    axes = ("seq", "head")
    while step < count:
        moved = jax.tree.map(lambda x: lax.ppermute(x, axes, order([(i, i + step) for i in range(count - step)])), state)
        has = (me < count - step) if reverse else (me >= step)
        f, m, n = state
        state = (
            jnp.where(has, f * moved[0], f),
            m + jnp.where(has, by_head(f) * moved[1], 0.0),
            n + jnp.where(has, f[:, None] * moved[2], 0.0),
        )
        step *= 2
    moved = [lax.ppermute(x, axes, order([(i, i + 1) for i in range(count - 1)])) for x in state[1:]]
    return moved[0].astype(BF), jnp.concatenate([moved[1], jnp.zeros_like(moved[1])], 0).astype(BF)


def bias_columns(gate_bias):
    hi = lax.reduce_precision(gate_bias, 8, 7)
    mid = lax.reduce_precision(gate_bias - hi, 8, 7)
    return jnp.stack([hi, mid, gate_bias - hi - mid], axis=1).astype(BF)


def gather_blocks(att, rest, seq):
    def gather(block):
        full = lax.all_gather(lax.all_gather(block, "seq", axis=0, tiled=True), "head", axis=0)
        return full.reshape(PAIRS, seq // 2, 2, full.shape[1] // seq, full.shape[2])

    return gather(att), gather(rest)


def gather_any(q, k, v, gate, vectors, bias, out, up, down, seq):
    D = q.shape[0] * seq

    def whole(w, rows, cols):
        w = lax.all_gather(w, rows, axis=0, tiled=True)
        return lax.all_gather(w, cols, axis=1, tiled=True)

    def panels(w):
        return w.reshape(D, PAIRS, w.shape[1] // PAIRS).transpose(1, 0, 2)

    grid = [panels(whole(w, "seq", "head")) for w in (q, k, v)]
    gates = panels(whole(gate, "seq", "head"))
    lines = [jnp.broadcast_to(lax.all_gather(w, "seq", tiled=True)[None, :, None], (PAIRS, D, 1)) for w in vectors]
    bias = bias_columns(lax.all_gather(bias, "head", tiled=True)).reshape(PAIRS, 1, 6)
    pad = jnp.zeros((PAIRS, D, LANES - 12), BF)
    ga = jnp.concatenate(grid + [gates] + lines + [jnp.broadcast_to(bias, (PAIRS, D, 6)), pad], axis=2)
    gf = [panels(whole(out, "head", "seq").T), panels(whole(up, "seq", "head")), panels(whole(down, "head", "seq").T)]
    gf = jnp.concatenate(gf, axis=2)
    shape = (PAIRS, seq // 2, 2, D // seq)
    return ga.reshape(shape + ga.shape[2:]), gf.reshape(shape + gf.shape[2:])


def scatter_blocks(gga, ggf):
    def scattered(x):
        x = x.reshape(PAIRS, -1, x.shape[-1]).astype(F32)
        x = lax.psum_scatter(x, "head", scatter_dimension=0, tiled=True)[0]
        return lax.psum_scatter(x, "seq", scatter_dimension=0, tiled=True)

    return scattered(gga), scattered(ggf)


def unpack(grad_a, grad_f, ff):
    block = lambda i: grad_a[:, i * LANES : (i + 1) * LANES]
    small = block(3)
    return (
        small[:, 2], small[:, 3], block(0), block(1), block(2), small[:, 0:2], small[0, 6:8] + small[0, 8:10],
        grad_f[:, :LANES].T, small[:, 4], small[:, 5], grad_f[:, LANES : LANES + ff], grad_f[:, LANES + ff :].T,
    )


def scatter_any(gga, ggf, ff):
    gga, ggf = (x.reshape(PAIRS, -1, x.shape[-1]).astype(F32) for x in (gga, ggf))

    def grid(x):
        x = x.transpose(1, 0, 2).reshape(x.shape[1], -1)
        x = lax.psum_scatter(x, "seq", scatter_dimension=0, tiled=True)
        return lax.psum_scatter(x, "head", scatter_dimension=1, tiled=True)

    block = lambda i: gga[:, :, i * LANES : (i + 1) * LANES]
    small = block(3)
    lines = lax.psum_scatter(lax.psum(small[0, :, 2:6], "head"), "seq", scatter_dimension=0, tiled=True)
    bias = (small[:, 0, 6:8] + small[:, 0, 8:10]).reshape(HEADS)
    bias = lax.psum_scatter(lax.psum(bias, "seq"), "head", scatter_dimension=0, tiled=True)
    return (
        lines[:, 0], lines[:, 1], grid(block(0)), grid(block(1)), grid(block(2)), grid(small[:, :, 0:2]), bias,
        grid(ggf[:, :, :LANES]).T, lines[:, 2], lines[:, 3], grid(ggf[:, :, LANES : LANES + ff]),
        grid(ggf[:, :, LANES + ff :]).T,
    )


def shards(
    tokens, lengths, feature_seed, norm_gain, norm_shift, query_weight, key_weight, value_weight, gate_weight, gate_bias,
    out_weight, ffn_gain, ffn_shift, up_weight, down_weight, cotangent,
):
    seq, head = lax.axis_size("seq"), lax.axis_size("head")
    T, D = tokens.shape
    rows = D // seq
    ff = up_weight.shape[1] * head // PAIRS
    base = here(T).astype(I32).reshape(1)
    by_pair = head == PAIRS
    vectors = (norm_gain, norm_shift, ffn_gain, ffn_shift)
    if by_pair:
        bias = jnp.broadcast_to(bias_columns(gate_bias).reshape(1, 6), (rows, 6))
        small = [gate_weight] + [w[:, None] for w in vectors] + [bias, jnp.zeros((rows, LANES - 12), BF)]
        att = jnp.concatenate([query_weight, key_weight, value_weight] + small, axis=1)
        ga, gf = gather_blocks(att, jnp.concatenate([out_weight.T, up_weight, down_weight.T], axis=1), seq)
    else:
        ga, gf = gather_any(query_weight, key_weight, value_weight, gate_weight, vectors, gate_bias, out_weight,
                            up_weight, down_weight, seq)
    specs = buffers(T, D, ATT, LANES + 2 * ff, ff, seq)
    args = (base, lengths, feature_seed, tokens, cotangent)
    state = {"ga": ga, "gf": gf}
    stage(lambda base, r: front(T, base, r), FRONT, specs, "front", args, state)
    state["min"], state["nin"] = scan_states(state["mem"], state["nrm"], state["total"], False)
    stage(lambda base, r: middle(T, base, r), MIDDLE, specs, "middle", args, state)
    state["aend"], state["bend"] = scan_states(state["adj"], state["bn"], state["total"], True)
    stage(lambda base, r: back(T, base, r, T * seq * head), BACK, specs, "back", args, state)
    if by_pair:
        weights = unpack(*scatter_blocks(state["gga"], state["ggf"]), ff)
    else:
        weights = scatter_any(state["gga"], state["ggf"], ff)
    return (state["result"], state["gtok"]) + weights


def solution(mesh):
    both, rows, grid = P(("seq", "head"), None), P("seq"), P("seq", "head")
    return jax.shard_map(
        shards,
        mesh=mesh,
        in_specs=(both, P(), P(), rows, rows, grid, grid, grid, grid, P("head"), P("head", "seq"), rows, rows, grid,
                  P("head", "seq"), both),
        out_specs=(both, both, rows, rows, grid, grid, grid, grid, P("head"), P("head", "seq"), rows, rows, grid,
                   P("head", "seq")),
        check_vma=False,
    )
```

time: 1500 us -> 669 us (0.45)
  blocking collectives: 345 us -> 36 us
  matrix products: 288 us -> 0 us
  local copies, waits for them, and re-layouts: 312 us -> 28.6 us
  other arithmetic: 138 us -> 19.8 us
  starting transfers between devices: 1 us -> 96.1 us
  Pallas kernels: 0 us -> 94.5 us
    dot_general x105 -> x0, matrix products: 283 us -> none  [the longest x16 65.4 us: block_step(): jnp.einsum('ihm,shm->ish', query_feat, key_feat, precision=highest)]
    all_gather x10 -> x1, blocking collectives: 282 us -> 36 us  [gather(): lax.all_gather(block, 'seq', axis=0, tiled=True)]
    psum x3 -> x0, waiting for transfers between devices: 147 us -> none  [the longest x1 85.6 us: shards(): lax.psum(jnp.dot(grad_hidden, full_up.T, preferred_element_type=jnp.float...]
    dynamic_update_slice x28 -> x0, local copies, waits for them, and re-layouts: 128 us -> none  [attention_part(): lax.scan(jax.checkpoint(block_step), start, xs)]
    ppermute x0 -> x32, waiting for transfers between devices: none -> 100 us  [the longest x28 97.6 us: scan_states(): lax.ppermute(x, axes, order([(i, i + step) for i in range(count - step)]))]
    ppermute x0 -> x32, starting transfers between devices: none -> 95.8 us  [the longest x28 90.5 us: scan_states(): lax.ppermute(x, axes, order([(i, i + step) for i in range(count - step)]))]
    pallas_call x0 -> x3, Pallas kernels: none -> 94.5 us  [stage(): pl.pallas_call(kernel, out_shape=[shape(n) for n in writes], in_specs=[sm...]
    unnamed x16 -> x8, waiting for transfers between devices: 1.44 us -> 67.2 us
  transfers between devices with their start and end apart: 15 -> 39, of which waited for: 8 -> 25; matrix products, arithmetic and copies ran while one was open for 34% -> 5% of each run, Pallas kernels for 0% -> 5%
where the time goes in v1:
time: 669 us; the launch traced here: 667 us
  waiting for transfers between devices  377 us (56%)
  starting transfers between devices  96.1 us (14%)
  Pallas kernels  94.5 us (14%)
  blocking collectives  36 us (5%)
  local copies, waits for them, and re-layouts  28.6 us (4%)
  other arithmetic  19.8 us (3%)
  between operations  15.4 us (2%)
    reduce_scatter x2, waiting for transfers between devices, scattered(): x = lax.psum_scatter(x, 'head', scatter_dimension=0, tiled=True)[0]  117 us
    ppermute x28, waiting for transfers between devices, scan_states(): lax.ppermute(x, axes, order([(i, i + step) for i in range(count - step)]))  97.6 us
    pallas_call x3, Pallas kernels, stage(): pl.pallas_call(kernel, out_shape=[shape(n) for n in writes], in_specs=[sm...  94.5 us
    ppermute x28, starting transfers between devices, scan_states(): lax.ppermute(x, axes, order([(i, i + step) for i in range(count - step)]))  90.5 us
    unnamed x8, waiting for transfers between devices  67.2 us
    reduce_scatter x1, waiting for transfers between devices, scattered(): return lax.psum_scatter(x, 'seq', scatter_dimension=0, tiled=True)  63.9 us
    all_gather x1, blocking collectives, gather(): lax.all_gather(block, 'seq', axis=0, tiled=True)  36 us
    all_gather x2, waiting for transfers between devices, gather(): lax.all_gather(lax.all_gather(block, 'seq', axis=0, tiled=True), 'head',...  22.1 us
  transfers between devices with their start and end apart: 39, of which 25 were waited for; matrix products, arithmetic and copies ran while one was open for 5% of the time, Pallas kernels for 5%

profile of v1, /device:TPU:0, one launch (start us, length us, event | category | flops | bytes accessed | tf_op | source)
XLA Modules:
  0.0 667.3 jit_solution(6510946091382208287)
XLA Ops:
  14.4 36.0 %all_gather.21 = bf16[512,512]{1,0:T(8,128)(2,1)} all-gather(bf16[64,512]{1,0:T(8,128)(2,1)S(1)} %concatenate.13), channel_id=1, replica_groups=mesh['seq'=8,'head'=4] {'seq'}, dimensions={0}, use_global_device_ids=true | all-gather | bytes 589824 | tf_op jit(solution)/shard_map/all_gather | solution.py:612
  50.5 6.8 %all-gather.6.cloned.1.call-done = bf16[512,1152]{1,0:T(8,128)(2,1)} async-done(((bf16[64,1152]{1,0:T(8,128)(2,1)}), bf16[512,1152]{1,0:T(8,128)(2,1)}) %all-gather.6.cloned.1.call-update) | async-done | bytes 1179664 | tf_op jit(solution)/shard_map/all_gather | solution.py:612
  58.1 22.1 %all-gather.10.cloned.1.call-done = bf16[2048,512]{1,0:T(8,128)(2,1)} async-done(((bf16[512,512]{1,0:T(8,128)(2,1)}), bf16[2048,512]{1,0:T(8,128)(2,1)}) %all-gather.10.cloned.1.call-update) | async-done | bytes 2097168 | tf_op jit(solution)/shard_map/all_gather | solution.py:612
  80.2 31.9 %front.1 = (f32[16,512]{1,0:T(8,128)}, f32[8,512]{1,0:T(8,128)}, bf16[512,512]{1,0:T(8,128)(2,1)}, f32[8,512]{1,0:T(8,128)}, f32[8,512]{1,0:T(8,128)}, /*index=5...) custom-call(s32[1]{0:T(128)} %bitcast.1.refs_0_, ...), custom_call_target="tpu_custom_call" | custom-call | tf_op jit(solution)/shard_map/front/pallas_call | solution.py:568
  117.9 9.0 %collective-permute-start.2 = (f32[4,128,256]{2,1,0:T(8,128)S(1)}, f32[4,128,256]{2,1,0:T(8,128)S(1)}, u32[]{:S(2)}, u32[]{:S(2)}) collective-permute-start(f32[4,128,256]{2,1,0:T(8,128)S(1)} %select_add_fusion.9), channel_id=1, source_target_pairs={{0,2},{1,3},{2,4},{3,5},{4,6},{5,7},{6,8},{7,9},{8,10},{9,11},{10,... | collective-permute-start | bytes 1572872 | tf_op jit(solution)/shard_map/ppermute | solution.py:591
  130.2 4.8 collective-permute-done.17
  135.3 3.3 collective-permute-done.2
  138.7 4.4 collective-permute-start.4
  143.1 3.4 collective-permute-start.3
  148.0 5.7 collective-permute-done.4
  153.8 8.2 %collective-permute-start.6 = (f32[4,128,256]{2,1,0:T(8,128)S(1)}, f32[4,128,256]{2,1,0:T(8,128)S(1)}, u32[]{:S(2)}, u32[]{:S(2)}) collective-permute-start(f32[4,128,256]{2,1,0:T(8,128)S(1)} %select_add_fusion.7), channel_id=1, source_target_pairs={{0,8},{1,9},{2,10},{3,11},{4,12},{5,13},{6,14},{7,15},{8,16},{9,17... | collective-permute-start | bytes 1572872 | tf_op jit(solution)/shard_map/ppermute | solution.py:591
  166.0 7.6 %collective-permute-start.7 = (f32[8]{0:T(128)S(1)}, f32[8]{0:T(128)S(1)}, u32[]{:S(2)}, u32[]{:S(2)}) collective-permute-start(f32[8]{0:T(128)S(1)} %broadcast_select_fusion.5), channel_id=1, source_target_pairs={{0,8},{1,9},{2,10},{3,11},{4,12},{5,13},{6,14},{7,15},{8,16},{9,17... | collective-permute-start | bytes 104 | tf_op jit(solution)/shard_map/ppermute | solution.py:591
  173.9 5.7 collective-permute-start.11
  186.2 7.6 %collective-permute-start.13 = (f32[8,256]{1,0:T(8,128)S(1)}, f32[8,256]{1,0:T(8,128)S(1)}, u32[]{:S(2)}, u32[]{:S(2)}) collective-permute-start(f32[8,256]{1,0:T(8,128)S(1)} %select_add_fusion.17), channel_id=1, source_target_pairs={{0,8},{1,9},{2,10},{3,11},{4,12},{5,13},{6,14},{7,15},{8,16},{9,17... | collective-permute-start | bytes 24584 | tf_op jit(solution)/shard_map/ppermute | solution.py:591
  195.3 15.0 %collective-permute-start.14 = (f32[8,256]{1,0:T(8,128)S(1)}, f32[8,256]{1,0:T(8,128)S(1)}, u32[]{:S(2)}, u32[]{:S(2)}) collective-permute-start(f32[8,256]{1,0:T(8,128)S(1)} %select_add_fusion.16), channel_id=1, source_target_pairs={{0,16},{1,17},{2,18},{3,19},{4,20},{5,21},{6,22},{7,23},{8,24},{9,... | collective-permute-start | bytes 24584 | tf_op jit(solution)/shard_map/ppermute | solution.py:591
  215.1 27.9 %middle.1 = (bf16[4,4,2,64,1152]{4,3,2,1,0:T(8,128)(2,1)}, bf16[512,512]{1,0:T(8,128)(2,1)}, f32[512,512]{1,0:T(8,128)}, f32[8,512]{1,0:T(8,128)}, f32[8,512]{1,...) custom-call(s32[1]{0:T(128)} %bitcast.1.refs_0_, s32[3]{0:T(128)} %refs_1_.5, ...), custom_call_target="tpu_custom_call" | custom-call | tf_op jit(solution)/shard_map/middle/pallas_call | solution.py:568
  245.3 3.8 collective-permute-done.16
  251.8 19.2 %collective-permute-done.18 = f32[4,128,256]{2,1,0:T(8,128)S(1)} collective-permute-done((f32[4,128,256]{2,1,0:T(8,128)S(1)}, f32[4,128,256]{2,1,0:T(8,128)S(1)}, u32[]{:S(2)}, u32[]{:S(2)}) %collective-permute-start.18) | collective-permute-done | bytes 524320 | tf_op jit(solution)/shard_map/ppermute | solution.py:591
  273.7 6.4 collective-permute-done.19
  281.7 6.4 collective-permute-done.20
  293.9 10.0 %collective-permute-done.22 = f32[4,128,256]{2,1,0:T(8,128)S(1)} collective-permute-done((f32[4,128,256]{2,1,0:T(8,128)S(1)}, f32[4,128,256]{2,1,0:T(8,128)S(1)}, u32[]{:S(2)}, u32[]{:S(2)}) %collective-permute-start.22) | collective-permute-done | bytes 524320 | tf_op jit(solution)/shard_map/ppermute | solution.py:591
  307.0 4.0 collective-permute-done.28
  312.3 19.4 %collective-permute-done.24 = f32[4,128,256]{2,1,0:T(8,128)S(1)} collective-permute-done((f32[4,128,256]{2,1,0:T(8,128)S(1)}, f32[4,128,256]{2,1,0:T(8,128)S(1)}, u32[]{:S(2)}, u32[]{:S(2)}) %collective-permute-start.24) | collective-permute-done | bytes 524320 | tf_op jit(solution)/shard_map/ppermute | solution.py:591
  334.5 9.0 %collective-permute-done.30 = f32[8,256]{1,0:T(8,128)S(1)} collective-permute-done((f32[8,256]{1,0:T(8,128)S(1)}, f32[8,256]{1,0:T(8,128)S(1)}, u32[]{:S(2)}, u32[]{:S(2)}) %collective-permute-start.30) | collective-permute-done | bytes 8224 | tf_op jit(solution)/shard_map/ppermute | solution.py:591
  348.0 34.7 %back.1 = (bf16[4,4,2,64,512]{4,3,2,1,0:T(8,128)(2,1)}, f32[512,512]{1,0:T(8,128)}) custom-call(s32[1]{0:T(128)} %bitcast.1.refs_0_, s32[3]{0:T(128)} %refs_1_.5, s32[1]{0:T(128)S(6)} %copy.72.refs_2_, bf16[512,512]{1,0:T(8,128)(2,1)} %refs_3_.5, bf16[512,512]{1,0:T(8,128)(2,1)} %refs_4_.5, bf16[4,4,2,64,512]{4,3,2,1,0:T(8,128)(2,1)} %bitcast.33, ...), custom_call_target="tpu_custom_call" | custom-call | tf_op jit(solution)/shard_map/back/pallas_call | solution.py:568
  382.7 4.2 bitcast_convert_fusion.1
  386.9 5.2 copy.56
  392.2 6.8 %bitcast_convert_fusion = f32[4,512,1152]{2,1,0:T(8,128)} fusion(bf16[4,4,2,64,1152]{4,3,2,1,0:T(8,128)(2,1)} %get-tuple-element.69), kind=kLoop, calls=%fused_computation | loop fusion | flops 2359296 | bytes 14155776 | tf_op jit(solution)/shard_map/convert_element_type | solution.py:642
  399.1 38.4 %reduce-scatter.7.cloned.1.call-done = f32[1,512,512]{1,2,0:T(8,128)} async-done(((f32[4,512,512]{1,2,0:T(8,128)}), f32[1,512,512]{1,2,0:T(8,128)}) %reduce-scatter.7.cloned.1.call-update) | async-done | bytes 1048592 | tf_op jit(solution)/shard_map/reduce_scatter | solution.py:643
  440.1 78.4 %reduce-scatter.9.cloned.1.call-done = f32[1,512,1152]{2,1,0:T(8,128)} async-done(((f32[4,512,1152]{2,1,0:T(8,128)}), f32[1,512,1152]{2,1,0:T(8,128)}) %reduce-scatter.9.cloned.1.call-update) | async-done | bytes 2359312 | tf_op jit(solution)/shard_map/reduce_scatter | solution.py:643
  518.5 67.1 %reduce-scatter.13.cloned.1.call-done = f32[64,512]{1,0:T(8,128)} async-done(((f32[512,512]{1,0:T(8,128)}), f32[64,512]{1,0:T(8,128)}) %reduce-scatter.13.cloned.1.call-update) | async-done | bytes 131088
  593.5 63.9 %reduce-scatter.11.cloned.1.call-done = f32[64,1152]{1,0:T(8,128)} async-done(((f32[512,1152]{1,0:T(8,128)}), f32[64,1152]{1,0:T(8,128)}) %reduce-scatter.11.cloned.1.call-update) | async-done | bytes 294928 | tf_op jit(solution)/shard_map/reduce_scatter | solution.py:644
  (157 shorter events, 75.7 us)
Async XLA Ops:
  7.2 50.2 %all-gather.6.cloned.1.call-start = ((), (), s32[]{:S(2)}) async-start(), calls=%async_computation.4 | async-start | bytes 1327104 | tf_op jit(solution)/shard_map/all_gather | solution.py:612
  8.8 71.4 %all-gather.10.cloned.1.call-start = ((), (), s32[]{:S(2)}) async-start(), calls=%async_computation.9 | async-start | bytes 2621440 | tf_op jit(solution)/shard_map/all_gather | solution.py:612
  50.5 163.9 %all-gather.8.cloned.1.call-start = ((), (), s32[]{:S(2)}) async-start(), calls=%async_computation.8 | async-start | bytes 5898240 | tf_op jit(solution)/shard_map/all_gather | solution.py:612
  57.4 380.0 %reduce-scatter.7.cloned.1.call-start = ((), (), s32[]{:S(2)}) async-start(), calls=%async_computation.5 | async-start | bytes 5242880 | tf_op jit(solution)/shard_map/reduce_scatter | solution.py:643
  117.9 20.6 %collective-permute-start.2 = (f32[4,128,256]{2,1,0:T(8,128)S(1)}, f32[4,128,256]{2,1,0:T(8,128)S(1)}, u32[]{:S(2)}, u32[]{:S(2)}) collective-permute-start(f32[4,128,256]{2,1,0:T(8,128)S(1)} %select_add_fusion.9), channel_id=1, source_target_pairs={{0,2},{1,3},{2,4},{3,5},{4,6},{5,7},{6,8},{7,9},{8,10},{9,11},{10,... | collective-permute-start | bytes 1572872 | tf_op jit(solution)/shard_map/ppermute | solution.py:591
  128.9 6.2 collective-permute-start.17
  138.7 15.0 %collective-permute-start.4 = (f32[4,128,256]{2,1,0:T(8,128)S(1)}, f32[4,128,256]{2,1,0:T(8,128)S(1)}, u32[]{:S(2)}, u32[]{:S(2)}) collective-permute-start(f32[4,128,256]{2,1,0:T(8,128)S(1)} %select_add_fusion.8), channel_id=1, source_target_pairs={{0,4},{1,5},{2,6},{3,7},{4,8},{5,9},{6,10},{7,11},{8,12},{9,13},{1... | collective-permute-start | bytes 1572872 | tf_op jit(solution)/shard_map/ppermute | solution.py:591
  143.1 4.7 collective-permute-start.3
  153.8 25.9 %collective-permute-start.6 = (f32[4,128,256]{2,1,0:T(8,128)S(1)}, f32[4,128,256]{2,1,0:T(8,128)S(1)}, u32[]{:S(2)}, u32[]{:S(2)}) collective-permute-start(f32[4,128,256]{2,1,0:T(8,128)S(1)} %select_add_fusion.7), channel_id=1, source_target_pairs={{0,8},{1,9},{2,10},{3,11},{4,12},{5,13},{6,14},{7,15},{8,16},{9,17... | collective-permute-start | bytes 1572872 | tf_op jit(solution)/shard_map/ppermute | solution.py:591
  162.0 11.9 %collective-permute-start.10 = (f32[8,256]{1,0:T(8,128)S(1)}, f32[8,256]{1,0:T(8,128)S(1)}, u32[]{:S(2)}, u32[]{:S(2)}) collective-permute-start(f32[8,256]{1,0:T(8,128)S(1)} %slice_convert_fusion.1), channel_id=1, source_target_pairs={{0,1},{1,2},{2,3},{3,4},{4,5},{5,6},{6,7},{7,8},{8,9},{9,10},{10,1... | collective-permute-start | bytes 24584 | tf_op jit(solution)/shard_map/ppermute | solution.py:591
  166.0 18.7 %collective-permute-start.7 = (f32[8]{0:T(128)S(1)}, f32[8]{0:T(128)S(1)}, u32[]{:S(2)}, u32[]{:S(2)}) collective-permute-start(f32[8]{0:T(128)S(1)} %broadcast_select_fusion.5), channel_id=1, source_target_pairs={{0,8},{1,9},{2,10},{3,11},{4,12},{5,13},{6,14},{7,15},{8,16},{9,17... | collective-permute-start | bytes 104 | tf_op jit(solution)/shard_map/ppermute | solution.py:591
  173.9 7.6 %collective-permute-start.11 = (f32[8,256]{1,0:T(8,128)S(1)}, f32[8,256]{1,0:T(8,128)S(1)}, u32[]{:S(2)}, u32[]{:S(2)}) collective-permute-start(f32[8,256]{1,0:T(8,128)S(1)} %select_add_fusion.19), channel_id=1, source_target_pairs={{0,2},{1,3},{2,4},{3,5},{4,6},{5,7},{6,8},{7,9},{8,10},{9,11},{10,... | collective-permute-start | bytes 24584 | tf_op jit(solution)/shard_map/ppermute | solution.py:591
  179.9 13.9 %collective-permute-start.8 = (f32[4,128,256]{2,1,0:T(8,128)S(1)}, f32[4,128,256]{2,1,0:T(8,128)S(1)}, u32[]{:S(2)}, u32[]{:S(2)}) collective-permute-start(f32[4,128,256]{2,1,0:T(8,128)S(1)} %select_add_fusion.6), channel_id=1, source_target_pairs={{0,16},{1,17},{2,18},{3,19},{4,20},{5,21},{6,22},{7,23},{8,24},{9,... | collective-permute-start | bytes 1572872 | tf_op jit(solution)/shard_map/ppermute | solution.py:591
  186.2 9.1 %collective-permute-start.13 = (f32[8,256]{1,0:T(8,128)S(1)}, f32[8,256]{1,0:T(8,128)S(1)}, u32[]{:S(2)}, u32[]{:S(2)}) collective-permute-start(f32[8,256]{1,0:T(8,128)S(1)} %select_add_fusion.17), channel_id=1, source_target_pairs={{0,8},{1,9},{2,10},{3,11},{4,12},{5,13},{6,14},{7,15},{8,16},{9,17... | collective-permute-start | bytes 24584 | tf_op jit(solution)/shard_map/ppermute | solution.py:591
  193.9 20.5 %collective-permute-start.9 = (bf16[4,128,256]{2,1,0:T(8,128)(2,1)S(1)}, bf16[4,128,256]{2,1,0:T(8,128)(2,1)S(1)}, u32[]{:S(2)}, u32[]{:S(2)}) collective-permute-start(bf16[4,128,256]{2,1,0:T(8,128)(2,1)S(1)} %select_add_fusion.5), channel_id=1, source_target_pairs={{0,1},{1,2},{2,3},{3,4},{4,5},{5,6},{6,7},{7,8},{8,9},{9,10},{10,1... | collective-permute-start | bytes 786440 | tf_op jit(solution)/shard_map/ppermute | solution.py:600
  195.3 16.3 %collective-permute-start.14 = (f32[8,256]{1,0:T(8,128)S(1)}, f32[8,256]{1,0:T(8,128)S(1)}, u32[]{:S(2)}, u32[]{:S(2)}) collective-permute-start(f32[8,256]{1,0:T(8,128)S(1)} %select_add_fusion.16), channel_id=1, source_target_pairs={{0,16},{1,17},{2,18},{3,19},{4,20},{5,21},{6,22},{7,23},{8,24},{9,... | collective-permute-start | bytes 24584 | tf_op jit(solution)/shard_map/ppermute | solution.py:591
  244.0 5.1 collective-permute-start.16
  250.2 20.8 %collective-permute-start.18 = (f32[4,128,256]{2,1,0:T(8,128)S(1)}, f32[4,128,256]{2,1,0:T(8,128)S(1)}, u32[]{:S(2)}, u32[]{:S(2)}) collective-permute-start(f32[4,128,256]{2,1,0:T(8,128)S(1)} %select_add_fusion.4), channel_id=1, source_target_pairs={{2,0},{3,1},{4,2},{5,3},{6,4},{7,5},{8,6},{9,7},{10,8},{11,9},{12,... | collective-permute-start | bytes 1572872 | tf_op jit(solution)/shard_map/ppermute | solution.py:591
  271.1 16.9 %collective-permute-start.20 = (f32[4,128,256]{2,1,0:T(8,128)S(1)}, f32[4,128,256]{2,1,0:T(8,128)S(1)}, u32[]{:S(2)}, u32[]{:S(2)}) collective-permute-start(f32[4,128,256]{2,1,0:T(8,128)S(1)} %select_add_fusion.3), channel_id=1, source_target_pairs={{4,0},{5,1},{6,2},{7,3},{8,4},{9,5},{10,6},{11,7},{12,8},{13,9},{1... | collective-permute-start | bytes 1572872 | tf_op jit(solution)/shard_map/ppermute | solution.py:591
  272.4 7.7 %collective-permute-start.19 = (f32[8]{0:T(128)S(1)}, f32[8]{0:T(128)S(1)}, u32[]{:S(2)}, u32[]{:S(2)}) collective-permute-start(f32[8]{0:T(128)S(1)} %get-tuple-element.123), channel_id=1, source_target_pairs={{2,0},{3,1},{4,2},{5,3},{6,4},{7,5},{8,6},{9,7},{10,8},{11,9},{12,... | collective-permute-start | bytes 104 | tf_op jit(solution)/shard_map/ppermute | solution.py:591
  280.1 10.7 %collective-permute-start.21 = (f32[8]{0:T(128)S(1)}, f32[8]{0:T(128)S(1)}, u32[]{:S(2)}, u32[]{:S(2)}) collective-permute-start(f32[8]{0:T(128)S(1)} %broadcast_select_fusion.2), channel_id=1, source_target_pairs={{4,0},{5,1},{6,2},{7,3},{8,4},{9,5},{10,6},{11,7},{12,8},{13,9},{1... | collective-permute-start | bytes 104 | tf_op jit(solution)/shard_map/ppermute | solution.py:591
  288.2 15.7 %collective-permute-start.22 = (f32[4,128,256]{2,1,0:T(8,128)S(1)}, f32[4,128,256]{2,1,0:T(8,128)S(1)}, u32[]{:S(2)}, u32[]{:S(2)}) collective-permute-start(f32[4,128,256]{2,1,0:T(8,128)S(1)} %select_add_fusion.2), channel_id=1, source_target_pairs={{8,0},{9,1},{10,2},{11,3},{12,4},{13,5},{14,6},{15,7},{16,8},{17,9... | collective-permute-start | bytes 1572872 | tf_op jit(solution)/shard_map/ppermute | solution.py:591
  290.8 15.9 %collective-permute-start.23 = (f32[8]{0:T(128)S(1)}, f32[8]{0:T(128)S(1)}, u32[]{:S(2)}, u32[]{:S(2)}) collective-permute-start(f32[8]{0:T(128)S(1)} %broadcast_select_fusion.1), channel_id=1, source_target_pairs={{8,0},{9,1},{10,2},{11,3},{12,4},{13,5},{14,6},{15,7},{16,8},{17,9... | collective-permute-start | bytes 104 | tf_op jit(solution)/shard_map/ppermute | solution.py:591
  292.6 12.7 %collective-permute-start.27 = (f32[8,256]{1,0:T(8,128)S(1)}, f32[8,256]{1,0:T(8,128)S(1)}, u32[]{:S(2)}, u32[]{:S(2)}) collective-permute-start(f32[8,256]{1,0:T(8,128)S(1)} %select_add_fusion.14), channel_id=1, source_target_pairs={{2,0},{3,1},{4,2},{5,3},{6,4},{7,5},{8,6},{9,7},{10,8},{11,9},{12,... | collective-permute-start | bytes 24584 | tf_op jit(solution)/shard_map/ppermute | solution.py:591
  304.0 27.7 %collective-permute-start.24 = (f32[4,128,256]{2,1,0:T(8,128)S(1)}, f32[4,128,256]{2,1,0:T(8,128)S(1)}, u32[]{:S(2)}, u32[]{:S(2)}) collective-permute-start(f32[4,128,256]{2,1,0:T(8,128)S(1)} %select_add_fusion.1), channel_id=1, source_target_pairs={{16,0},{17,1},{18,2},{19,3},{20,4},{21,5},{22,6},{23,7},{24,8},{25... | collective-permute-start | bytes 1572872 | tf_op jit(solution)/shard_map/ppermute | solution.py:591
  305.4 5.5 collective-permute-start.28
  311.0 22.1 %collective-permute-start.29 = (f32[8,256]{1,0:T(8,128)S(1)}, f32[8,256]{1,0:T(8,128)S(1)}, u32[]{:S(2)}, u32[]{:S(2)}) collective-permute-start(f32[8,256]{1,0:T(8,128)S(1)} %select_add_fusion.12), channel_id=1, source_target_pairs={{8,0},{9,1},{10,2},{11,3},{12,4},{13,5},{14,6},{15,7},{16,8},{17,9... | collective-permute-start | bytes 24584 | tf_op jit(solution)/shard_map/ppermute | solution.py:591
  331.9 15.4 %collective-permute-start.25 = (bf16[4,128,256]{2,1,0:T(8,128)(2,1)S(1)}, bf16[4,128,256]{2,1,0:T(8,128)(2,1)S(1)}, u32[]{:S(2)}, u32[]{:S(2)}) collective-permute-start(bf16[4,128,256]{2,1,0:T(8,128)(2,1)S(1)} %select_add_fusion), channel_id=1, source_target_pairs={{1,0},{2,1},{3,2},{4,3},{5,4},{6,5},{7,6},{8,7},{9,8},{10,9},{11,1... | collective-permute-start | bytes 786440 | tf_op jit(solution)/shard_map/ppermute | solution.py:600
  333.3 10.3 %collective-permute-start.30 = (f32[8,256]{1,0:T(8,128)S(1)}, f32[8,256]{1,0:T(8,128)S(1)}, u32[]{:S(2)}, u32[]{:S(2)}) collective-permute-start(f32[8,256]{1,0:T(8,128)S(1)} %select_add_fusion.11), channel_id=1, source_target_pairs={{16,0},{17,1},{18,2},{19,3},{20,4},{21,5},{22,6},{23,7},{24,8},{25... | collective-permute-start | bytes 24584 | tf_op jit(solution)/shard_map/ppermute | solution.py:591
  392.2 126.3 %reduce-scatter.9.cloned.1.call-start = ((), (), s32[]{:S(2)}) async-start(), calls=%async_computation.6 | async-start | bytes 11796480 | tf_op jit(solution)/shard_map/reduce_scatter | solution.py:643
  399.0 186.5 %reduce-scatter.13.cloned.1.call-start = ((), (), s32[]{:S(2)}) async-start(), calls=%async_computation.10 | async-start | bytes 1179648
  440.0 217.4 %reduce-scatter.11.cloned.1.call-start = ((), (), s32[]{:S(2)}) async-start(), calls=%async_computation.7 | async-start | bytes 2654208 | tf_op jit(solution)/shard_map/reduce_scatter | solution.py:644
  (11 other events, 120.0 us)
Sparse Core Ops, SparseCore 0:
  10.8 46.5 all-gather.5
  58.9 21.2 all-gather.9
  81.8 37.4 all-gather.7
  392.3 45.0 reduce-scatter.6
  440.1 78.3 reduce-scatter.8
  522.1 63.4 reduce-scatter.12
  589.1 68.2 reduce-scatter.10

commit v2 on v1

v2 whole, which is shorter than its diff:
```python
import functools
import math

import jax
import jax.numpy as jnp
from jax import lax
from jax.experimental import pallas as pl
from jax.experimental.pallas import tpu as pltpu
from jax.sharding import PartitionSpec as P

BF, F32, I32 = jnp.bfloat16, jnp.float32, jnp.int32
MESH = pl.DeviceIdType.MESH
HEADS, HEAD_DIM, FEATS = 8, 64, 128
PAIRS = HEADS // 2
LANES = 128
EPS, FLOOR2, GATE_PEN = 1e-5, 0.0625, 0.5
TABLE_SCALE = 1.0 / math.sqrt(21845.0)
FEAT_SCALE = 1.0 / math.sqrt(FEATS)
INV_TWO_PI, TWO_PI = 1.0 / (2.0 * math.pi), 2.0 * math.pi
SIN = (0.9999996027571254, -0.16666553170295112, 0.008332405799301931, -0.00019808693226998236,
       2.6997700314773084e-06, -2.036409109746239e-08)
COS = (0.9999992193982472, -0.4999942543676011, 0.04165980908449851, -0.0013858873219640337,
       2.420384320646774e-05, -2.1976364824224383e-07)
ERFC = (0.254829592, -0.284496736, 1.421413741, -1.453152027, 1.061405429)
ATT = 4 * LANES
KV, SMALL, QUERY = slice(0, 2 * LANES), slice(2 * LANES, 3 * LANES), slice(3 * LANES, 4 * LANES)
NORMAL, DECAY, STATE_ROWS = HEAD_DIM, HEAD_DIM + 1, HEAD_DIM + 8
STATES = (HEADS, STATE_ROWS, 2 * FEATS)
VMEM_BYTES = 56 * 1024 * 1024
LAYER_BYTES = 63 * 1024 * 1024


def nn(a, b):
    return lax.dot_general(a, b, (((1,), (0,)), ((), ())), preferred_element_type=F32)


def nt(a, b):
    return lax.dot_general(a, b, (((1,), (1,)), ((), ())), preferred_element_type=F32)


def tn(a, b):
    return lax.dot_general(a, b, (((0,), (0,)), ((), ())), preferred_element_type=F32)


def halves(x, axis=1):
    hi = x.astype(BF)
    return jnp.concatenate([hi, (x - hi.astype(F32)).astype(BF)], axis=axis)


def iota(shape, dim):
    return lax.broadcasted_iota(I32, shape, dim)


def rows_loop(total, step, body):
    step = min(step, total)

    def one(i, carry):
        body(pl.ds(pl.multiple_of(i * step, step), step), i * step, step)
        return carry

    lax.fori_loop(0, total // step, one, 0)


def pair_loop(body):
    def one(p, carry):
        body(p)
        return carry

    lax.fori_loop(0, PAIRS, one, 0)


def head_ones(rows, cols, row_span, col_span):
    same = (iota((rows, cols), 0) // row_span) % 2 == iota((rows, cols), 1) // col_span
    return jnp.where(same, 1.0, 0.0).astype(BF)


def marks(pos, base, lengths_ref):
    start = jnp.int32(0)
    segment = jnp.zeros(pos.shape, I32)
    reset = jnp.zeros(pos.shape, F32)
    carry = jnp.ones(pos.shape, F32)
    for d in range(lengths_ref.shape[0]):
        segment = segment + jnp.where(pos >= start, 1, 0)
        reset = jnp.where(pos == start, 1.0, reset)
        carry = jnp.where((pos >= start) & (pos - start <= pos - base), 0.0, carry)
        start = start + lengths_ref[d]
    live = jnp.where(pos < start, 1.0, 0.0)
    segment = segment + jnp.where(pos >= start, 1, 0)
    return segment, reset, live, carry, start


def horner(coefs, t):
    acc = jnp.full_like(t, coefs[-1])
    for c in coefs[-2::-1]:
        acc = acc * t + c
    return acc


def sincos(angle):
    r = angle - jnp.round(angle * INV_TWO_PI) * TWO_PI
    t = r * r
    return r * horner([c * FEAT_SCALE for c in SIN], t), horner([c * FEAT_SCALE for c in COS], t)


def gelu_parts(x):
    t = 1.0 / (1.0 + (0.3275911 / math.sqrt(2.0)) * jnp.abs(x))
    e = jnp.exp(-0.5 * x * x)
    q = 0.5 * t * horner(ERFC, t) * e
    cdf = jnp.where(x < 0.0, q, 1.0 - q)
    return x * cdf, cdf + x * e * (1.0 / math.sqrt(2.0 * math.pi))


def norm_stats(x):
    center = jnp.mean(x, axis=-1, keepdims=True)
    spread = jnp.mean(x * x, axis=-1, keepdims=True) - center * center
    inv = lax.rsqrt(spread + EPS)
    return (x - center) * inv, inv


def norm_back(grad, xhat, inv, gain):
    p = grad * gain
    return inv * (p - jnp.mean(p, axis=-1, keepdims=True) - xhat * jnp.mean(p * xhat, axis=-1, keepdims=True))


def by_eight(x):
    return jnp.sum(x.reshape(x.shape[0] // 8, 8, x.shape[1]), axis=0)


def panel(ref, p, cols):
    x = ref[p, :, :, :, cols]
    return x.reshape(x.shape[0] * x.shape[1] * x.shape[2], x.shape[3])


def low_lanes(rows):
    return iota((rows, LANES), 1) < HEAD_DIM


def widen(pair, a):
    return pair[:, a * HEAD_DIM : a * HEAD_DIM + 1]


def head_values(v, a, low):
    one = jnp.ones_like(v)
    return jnp.where(low, v, one) if a == 0 else jnp.where(low, one, v)


def state_of(states, p, a):
    own = states[2 * p + a, 0:HEAD_DIM, :]
    rest = jnp.broadcast_to(states[2 * p + a, NORMAL : NORMAL + 1, :], own.shape)
    return jnp.concatenate([own, rest] if a == 0 else [rest, own], axis=0)


def put_state(states, h, own, normal, decay):
    states[h, 0:HEAD_DIM, :] = own
    rest = jnp.zeros((STATE_ROWS - DECAY - 1, 2 * FEATS), F32)
    states[h, NORMAL:, :] = jnp.concatenate([normal, twice(decay), rest], axis=0)


def twice(x):
    return jnp.concatenate([x, x], axis=1)


def run_pairs(body, hook):
    def one(p):
        body(p)
        for at, act in (hook or {}).items():
            pl.when(p == at)(act)

    pair_loop(one)


def tables(T, base, r):
    pos = base + iota((8, T), 1)
    seg_row, _, live_row, _, _ = marks(pos, base, r.lengths)
    seg1, live1, pos1 = seg_row[0:1], live_row[0:1], pos[0:1]

    def mask_rows(rows, at, n):
        row_pos = base + at + iota((n, 1), 0)
        seg_col = marks(row_pos, base, r.lengths)[0]
        allowed = (seg_col == seg1) & (pos1 <= row_pos) & (live1 > 0.0)
        r.mask[rows, :] = jnp.where(allowed, 0.0, -1e30)

    rows_loop(T, 64, mask_rows)
    hash_seed = r.seed[0] * jnp.int32(-2048144789)

    def table(p):
        place = (p * LANES + iota((LANES, LANES), 0)) * FEATS + iota((LANES, LANES), 1)
        y = place * jnp.int32(-1640531535) + hash_seed
        y = y ^ lax.shift_right_logical(y, jnp.int32(15))
        y = y * jnp.int32(739982445)
        y = y ^ lax.shift_right_logical(y, jnp.int32(13))
        y = y * jnp.int32(695872825)
        y = y ^ lax.shift_right_logical(y, jnp.int32(16))
        s = jnp.full(y.shape, -510, I32)
        for k in range(4):
            s = s + (lax.shift_right_logical(y, jnp.int32(8 * k)) & jnp.int32(255))
        top = iota((LANES, LANES), 0) < HEAD_DIM
        odd = s & 1

        def diagonal(x):
            x = x.astype(F32)
            return jnp.concatenate([jnp.where(top, x, 0.0), jnp.where(top, 0.0, x)], axis=1).astype(BF)

        r.tab[p, 0:LANES, :] = diagonal(s - odd)
        r.tab[p, LANES:, :] = diagonal(odd)
        r.tabn[p] = diagonal(s)

    pair_loop(table)


def first_norm(T, base, r):
    pick = jnp.where(iota((16, LANES), 0) == iota((16, LANES), 1), 1.0, 0.0).astype(BF)
    for p in range(PAIRS):
        rows = nt(pick, panel(r.ga, p, SMALL))
        r.gate[2 * p : 2 * p + 2, :] = rows[0:2]
        r.gate[8 + 2 * p : 10 + 2 * p, :] = rows[0:2]
        r.bias[2 * p : 2 * p + 1, :] = rows[6:7] + rows[7:8] + rows[8:9]
        r.bias[2 * p + 1 : 2 * p + 2, :] = rows[9:10] + rows[10:11] + rows[11:12]
        if p == 0:
            r.vec[...] = rows[0:8]

    def norm_rows(rows, at, n):
        xhat, _ = norm_stats(r.tok[rows, :].astype(F32))
        r.normed[rows, :] = (xhat * r.vec[2:3, :] + r.vec[3:4, :]).astype(BF)

    rows_loop(T, 64, norm_rows)
    logits = nt(r.gate[...].astype(BF), r.normed[...])[0:8] + r.bias[:, 0:1]
    r.logits[...] = logits
    pos = base + iota((8, T), 1)
    _, reset_row, live_row, carry_row, _ = marks(pos, base, r.lengths)
    decay = -(jnp.log1p(jnp.exp(-jnp.abs(logits))) + jnp.maximum(-logits, 0.0)) * live_row * (1.0 - reset_row)
    run = decay
    lane = iota((8, T), 1)
    shift = 1
    while shift < T:
        run = run + jnp.where(lane >= shift, pltpu.roll(run, shift, 1), 0.0)
        shift *= 2
    r.run[...] = run
    r.total[...] = jnp.broadcast_to(jnp.exp(run[:, T - 1 : T]) * carry_row[:, T - 1 : T], (8, LANES))
    hi = run.astype(BF).astype(F32)
    mid = (run - hi).astype(BF).astype(F32)
    run3 = jnp.concatenate([hi, mid, run - hi - mid, jnp.zeros_like(hi)], axis=0).astype(BF)

    def spread(p):
        chosen = iota((32, LANES), 0) % 8 == 2 * p + iota((32, LANES), 1) // HEAD_DIM
        r.rb[p] = tn(run3, jnp.where(chosen, 1.0, 0.0).astype(BF))

    pair_loop(spread)


def features(T, r, p, u, out):
    ones2 = head_ones(2 * LANES, 2 * LANES, HEAD_DIM, LANES)
    r.s1[...] = nn(jnp.concatenate([u, u], axis=1), r.tab[p])
    uf = u.astype(F32)
    r.s2[...] = nn(halves(uf * uf), ones2)

    def body(rows, at, n):
        s, c = sincos(r.s1[rows, :] * (lax.rsqrt(r.s2[rows, :] + 1e-6) * TABLE_SCALE))
        for a in range(2):
            out[2 * p + a, rows, 0:FEATS] = s[:, a * FEATS : (a + 1) * FEATS].astype(BF)
            out[2 * p + a, rows, FEATS : 2 * FEATS] = c[:, a * FEATS : (a + 1) * FEATS].astype(BF)

    rows_loop(T, 64, body)


def end_factor(T, base, r):
    last_seg = marks(base + T - 1 + iota((8, LANES), 1) * 0, base, r.lengths)[0][0:1, 0:1]
    seg_col, _, live_col, _, _ = marks(base + iota((T, LANES), 0), base, r.lengths)
    return jnp.where(seg_col == last_seg, live_col, 0.0)


def keys(T, base, r, hook=None):
    low = low_lanes(T)
    end_live = end_factor(T, base, r)

    def pair(p):
        kv = nn(r.normed[...], panel(r.ga, p, KV)).astype(BF)
        r.k[p] = kv[:, 0:LANES]
        r.v[p] = kv[:, LANES:]
        features(T, r, p, r.k[p], r.kf)
        decay_end = jnp.exp(r.rb[p, T - 1 : T, :] - r.rb[p]) * end_live
        four = [decay_end[:, 0:1], decay_end[:, 0:1], decay_end[:, HEAD_DIM : HEAD_DIM + 1], decay_end[:, HEAD_DIM : HEAD_DIM + 1]]
        lane = iota((T, LANES), 1)
        first = jnp.where(lane < 2, four[0], four[2])
        rough = first.astype(BF).astype(F32)
        first = jnp.where(lane % 2 == 0, rough, first - rough)
        ends = tn(first.astype(BF), jnp.concatenate([r.kf[2 * p], r.kf[2 * p + 1]], axis=1))
        for a in range(2):
            h = 2 * p + a
            scaled = (r.kf[h].astype(F32) * widen(decay_end, a)).astype(BF)
            state = tn(r.v[p], scaled)[a * HEAD_DIM : (a + 1) * HEAD_DIM]
            normal = ends[2 * a : 2 * a + 1, a * 2 * FEATS : (a + 1) * 2 * FEATS]
            normal = normal + ends[2 * a + 1 : 2 * a + 2, a * 2 * FEATS : (a + 1) * 2 * FEATS]
            put_state(r.out, h, state, normal, r.total[pl.ds(h, 1), :])

    run_pairs(pair, hook)


def queries(T, base, r, hook=None):
    low = low_lanes(T)

    def pair(p):
        r.q[p] = nn(r.normed[...], panel(r.ga, p, QUERY)).astype(BF)
        features(T, r, p, r.q[p], r.qf)
        v = r.v[p]
        for a in range(2):
            h = 2 * p + a
            r.s[...] = nt(r.qf[h], r.kf[h])
            run_row = r.run[pl.ds(h, 1), :]

            def body(rows, at, n):
                gap = jnp.minimum(widen(r.rb[p, rows, :], a) - run_row, r.mask[rows, :])
                w = r.s[rows, :] * jnp.exp(gap)
                rounded = w.astype(BF)
                r.w[h, rows, :] = rounded
                rest = jnp.sum(w - rounded.astype(F32), axis=1, keepdims=True)
                r.zfix[p, rows, a * HEAD_DIM : (a + 1) * HEAD_DIM] = jnp.broadcast_to(rest, (n, HEAD_DIM)).astype(BF)

            rows_loop(T, 64, body)
            r.own[h] = nn(r.w[h], head_values(v, a, low))

    run_pairs(pair, hook)


def carry_factor(T, base, r):
    _, _, live_col, carry_col, _ = marks(base + iota((T, LANES), 0), base, r.lengths)
    return live_col, carry_col


def attend(T, base, r):
    low = low_lanes(T)
    live_col, carry_col = carry_factor(T, base, r)

    def join(p):
        factor = jnp.exp(r.rb[p]) * carry_col
        total = []
        for a in range(2):
            h = 2 * p + a
            carried = nt(twice(r.qf[h]), halves(state_of(r.inn, p, a)))
            joined = r.own[h] + widen(factor, a) * carried
            r.joined[h] = joined
            total.append(joined)
        num = jnp.where(low, total[0], total[1])
        z = pltpu.roll(jnp.where(low, total[1], total[0]), HEAD_DIM, 1) + r.zfix[p].astype(F32)
        r.att[p] = (live_col * num * lax.rsqrt(z * z + FLOOR2)).astype(BF)

    pair_loop(join)
    o = slice(0, LANES)
    branch = None
    for p in range(0, PAIRS, 2):
        part = nt(
            jnp.concatenate([r.att[p], r.att[p + 1]], axis=1),
            jnp.concatenate([panel(r.gf, p, o), panel(r.gf, p + 1, o)], axis=1),
        )
        branch = part if branch is None else branch + part
    r.mid[...] = branch

    def norm_rows(rows, at, n):
        mid = r.mid[rows, :] + r.tok[rows, :].astype(F32)
        r.mid[rows, :] = mid
        xhat, inv = norm_stats(mid)
        r.xhat[rows, :] = xhat
        r.inv[rows, :] = jnp.broadcast_to(inv, (n, LANES))
        r.two[rows, :] = (xhat * r.vec[4:5, :] + r.vec[5:6, :]).astype(BF)

    rows_loop(T, 64, norm_rows)


def feed_columns(r):
    ff = (r.gf.shape[-1] - LANES) // 2
    return slice(LANES, LANES + ff), slice(LANES + ff, LANES + 2 * ff)


def feed(T, base, r):
    low = low_lanes(T)
    live_col, carry_col = carry_factor(T, base, r)
    r.acc1[...] = jnp.zeros_like(r.acc1)
    r.acc2[...] = jnp.zeros_like(r.acc2)
    u, d = feed_columns(r)
    o = slice(0, LANES)

    def part(p):
        up, down = panel(r.gf, p, u), panel(r.gf, p, d)
        r.h1[...] = nn(r.two[...], up)
        r.h2[...] = nn(r.cot[...], down)

        def body(rows, at, n):
            value, slope = gelu_parts(r.h1[rows, :])
            r.act[p, rows, :] = value.astype(BF)
            r.gh[p, rows, :] = (r.h2[rows, :] * slope).astype(BF)

        rows_loop(T, 64, body)
        r.acc1[...] += nt(r.act[p], down)
        r.acc2[...] += nt(r.gh[p], up)

    pair_loop(part)
    r.sums[...] = jnp.zeros_like(r.sums)

    def finish(rows, at, n):
        r.result[rows, :] = (r.mid[rows, :] + r.acc1[rows, :]).astype(BF)
        xhat, gn = r.xhat[rows, :], r.acc2[rows, :]
        r.sums[0:8, :] += by_eight(gn * xhat)
        r.sums[8:16, :] += by_eight(gn)
        back = norm_back(gn, xhat, r.inv[rows, 0:1], r.vec[4:5, :])
        grad = r.cot[rows, :].astype(F32) + back
        r.gmid[rows, :] = grad
        r.gb[rows, :] = grad.astype(BF)

    rows_loop(T, 64, finish)
    r.fsum[0:1, :] = jnp.sum(r.sums[0:8, :], axis=0, keepdims=True)
    r.fsum[1:2, :] = jnp.sum(r.sums[8:16, :], axis=0, keepdims=True)
    ones1 = head_ones(2 * LANES, LANES, HEAD_DIM, HEAD_DIM)
    row_ones = jnp.ones((16, 2 * LANES), BF)
    first_half = iota((T, LANES), 1) % HEAD_DIM < HEAD_DIM // 2

    def back(p):
        g = nn(r.gb[...], panel(r.gf, p, o)).astype(BF).astype(F32) * live_col
        total = [r.joined[2 * p], r.joined[2 * p + 1]]
        num = jnp.where(low, total[0], total[1])
        z = pltpu.roll(jnp.where(low, total[1], total[0]), HEAD_DIM, 1) + r.zfix[p].astype(F32)
        rden = lax.rsqrt(z * z + FLOOR2)
        dn = (g * rden).astype(BF).astype(F32)
        dz = nn(halves(dn * num), ones1) * (z * rden * rden)
        dz = pltpu.roll(dz * (-2.0 / HEAD_DIM), HEAD_DIM, 1)
        rough = dz.astype(BF).astype(F32)
        dz = jnp.where(first_half, rough, dz - rough)
        factor = jnp.exp(r.rb[p]) * carry_col
        for a in range(2):
            h = 2 * p + a
            joint = (jnp.where(low, dn, dz) if a == 0 else jnp.where(low, dz, dn)).astype(BF)
            r.dn[h] = joint
            r.dr[pl.ds(h, 1), :] = nt(row_ones, halves(joint.astype(F32) * total[a]))[0:1]
            adj = tn(joint, (r.qf[h].astype(F32) * widen(factor, a)).astype(BF))
            at, half = (1 - a) * HEAD_DIM, HEAD_DIM // 2
            normal = 0.5 * (adj[at : at + 1] + adj[at + half : at + half + 1])
            put_state(r.adj, h, adj[a * HEAD_DIM : (a + 1) * HEAD_DIM], normal, r.total[pl.ds(h, 1), :])

    pair_loop(back)


def feed_grads(T, base, r, hook=None):
    u, d = feed_columns(r)

    def part(p):
        put_panel(r.ggf, p, u, tn(r.two[...], r.gh[p]))
        put_panel(r.ggf, p, d, tn(r.cot[...], r.act[p]))
        put_panel(r.ggf, p, slice(0, LANES), tn(r.gb[...], r.att[p]))

    run_pairs(part, hook)


def put_panel(ref, p, cols, x):
    shape = ref.shape[1:4] + (x.shape[1],)
    ref[p, :, :, :, cols] = x.astype(BF).reshape(shape)


def back(T, base, r, tokens_all, near_hook=None, between=lambda: None, far_hook=None):
    D = r.tok.shape[1]
    low = low_lanes(T)
    _, carry_col = carry_factor(T, base, r)
    end_live = end_factor(T, base, r)
    ones1 = head_ones(2 * LANES, LANES, HEAD_DIM, HEAD_DIM)
    row_ones = jnp.ones((16, 2 * LANES), BF)
    r.acc1[...] = jnp.zeros_like(r.acc1)

    def feature_back(p, u, da):
        ds = nt(da, r.tabn[p]) * TABLE_SCALE
        uf = u.astype(F32)
        inv = lax.rsqrt(nn(halves(uf * uf), ones1) + 1e-6)
        uh = uf * inv
        return (inv * (ds - uh * nn(halves(uh * ds), ones1))).astype(BF)

    def angles(rows, source, feat, h):
        x, f = source[rows, :], feat[h, rows, :].astype(F32)
        return x[:, :FEATS] * f[:, FEATS:] - x[:, FEATS:] * f[:, :FEATS]

    def near(p):
        v = r.v[p]
        factor = jnp.exp(r.rb[p]) * carry_col
        for a in range(2):
            h = 2 * p + a
            r.s[...] = nt(r.dn[h], head_values(v, a, low))
            run_row = r.run[pl.ds(h, 1), :]

            def body(rows, at, n):
                gap = jnp.minimum(widen(r.rb[p, rows, :], a) - run_row, r.mask[rows, :])
                r.ds[rows, :] = (r.s[rows, :] * jnp.exp(gap)).astype(BF)

            rows_loop(T, 64, body)
            before = halves(state_of(r.inn, p, a), 0)
            r.s1[...] = nn(r.ds[...], r.kf[h]) + widen(factor, a) * nn(twice(r.dn[h]), before)
            r.s2[...] = tn(r.ds[...], r.qf[h])
            r.ghv[h] = tn(r.w[h], r.dn[h])

            def turn(rows, at, n):
                r.da[p, rows, a * FEATS : (a + 1) * FEATS] = angles(rows, r.s1, r.qf, h).astype(BF)
                r.da[p, rows, (2 + a) * FEATS : (3 + a) * FEATS] = angles(rows, r.s2, r.kf, h).astype(BF)

            rows_loop(T, 64, turn)

    def far(p):
        v = r.v[p]
        decay_end = jnp.exp(r.rb[p, T - 1 : T, :] - r.rb[p]) * end_live
        grad_v = []
        for a in range(2):
            h = 2 * p + a
            end, hv = state_of(r.aend, p, a), head_values(v, a, low)
            late = widen(decay_end, a) * nt(twice(r.kf[h]), halves(end))
            r.s2[...] = widen(decay_end, a) * nn(twice(hv), halves(end, 0))
            grad_hv = r.ghv[h] + late
            grad_v.append(grad_hv)

            def turn(rows, at, n):
                lanes = slice((2 + a) * FEATS, (3 + a) * FEATS)
                r.da[p, rows, lanes] = (r.da[p, rows, lanes].astype(F32) + angles(rows, r.s2, r.kf, h)).astype(BF)

            rows_loop(T, 64, turn)
            hvf = hv.astype(F32)
            k_side = nt(row_ones, halves(hvf * grad_hv))
            r.drun[pl.ds(h, 1), :] = r.dr[pl.ds(h, 1), :] - k_side[0:1]
            owed = jnp.sum(end * state_of(r.inn, p, a), axis=0, keepdims=True)
            owed = r.total[pl.ds(h, 1), 0:1] * jnp.sum(owed, axis=1, keepdims=True)
            owed = owed + jnp.sum(jnp.sum(hvf * late, axis=0, keepdims=True), axis=1, keepdims=True)
            r.owed[pl.ds(h, 1), :] = jnp.broadcast_to(owed, (1, LANES))
        grads = jnp.concatenate(
            [
                feature_back(p, r.k[p], r.da[p, :, 2 * FEATS :]),
                jnp.where(low, grad_v[0], grad_v[1]).astype(BF),
                feature_back(p, r.q[p], r.da[p, :, : 2 * FEATS]),
            ],
            axis=1,
        )
        weights = jnp.concatenate([panel(r.ga, p, KV), panel(r.ga, p, QUERY)], axis=1)
        r.acc1[...] += nt(grads, weights)
        put_panel(r.gga, p, slice(0, 3 * LANES), tn(r.normed[...], grads))

    run_pairs(near, near_hook)
    between()
    run_pairs(far, far_hook)
    pos = base + iota((8, T), 1)
    _, reset_row, live_row, _, filled = marks(pos, base, r.lengths)
    lane = iota((8, T), 1)
    run = r.drun[...]
    shift = 1
    while shift < T:
        run = run + jnp.where(lane < T - shift, pltpu.roll(run, T - shift, 1), 0.0)
        shift *= 2
    grad_decay = run + r.owed[:, 0:1]
    logits = r.logits[...]
    e = jnp.exp(-jnp.abs(logits))
    small, large = e / (1.0 + e), 1.0 / (1.0 + e)
    gate = jnp.where(logits >= 0.0, large, small)
    rest = jnp.where(logits >= 0.0, small, large)
    penalty = GATE_PEN * tokens_all / HEADS / jnp.broadcast_to(filled, (8, T)).astype(F32)
    grad_logits = grad_decay * live_row * (1.0 - reset_row) * rest + penalty * live_row * gate * rest
    both = halves(grad_logits, 0)
    r.acc1[...] += tn(both, r.gate[...].astype(BF))
    gate_rows = nn(both, r.normed[...])
    gate_rows = gate_rows[0:8] + gate_rows[8:16]
    bias = jnp.broadcast_to(jnp.sum(grad_logits, axis=1, keepdims=True), (8, D))
    r.sums[...] = jnp.zeros_like(r.sums)

    def finish(rows, at, n):
        xhat, inv = norm_stats(r.tok[rows, :].astype(F32))
        gn = r.acc1[rows, :]
        r.sums[0:8, :] += by_eight(gn * xhat)
        r.sums[8:16, :] += by_eight(gn)
        r.gtok[rows, :] = r.gmid[rows, :] + norm_back(gn, xhat, inv, r.vec[2:3, :])

    rows_loop(T, 64, finish)
    norm_gain = jnp.sum(r.sums[0:8, :], axis=0, keepdims=True)
    norm_shift = jnp.sum(r.sums[8:16, :], axis=0, keepdims=True)
    lines = [norm_gain, norm_shift, r.fsum[0:2, :]]
    for p in range(PAIRS):
        rows = jnp.concatenate([gate_rows[2 * p : 2 * p + 2]] + lines + [bias[2 * p : 2 * p + 2]], axis=0)
        for g in range(D // LANES):
            r.lines[p, g] = rows[:, g * LANES : (g + 1) * LANES]


class Refs:
    def __init__(self, **refs):
        self.__dict__.update(refs)


def buffers(T, D, att, rest, ff, seq):
    z = (PAIRS, seq // 2, 2, D // seq)
    pair = (PAIRS, T, LANES)
    return {
        "ga": (z + (att,), BF), "gf": (z + (rest,), BF), "gga": (z + (att - LANES,), BF), "ggf": (z + (rest,), BF),
        "gate": ((16, D), F32), "bias": ((8, D), F32), "vec": ((8, D), F32), "normed": ((T, D), BF),
        "logits": ((8, T), F32), "run": ((8, T), F32), "total": ((8, LANES), F32), "mask": ((T, T), F32),
        "s1": ((T, 2 * FEATS), F32), "s2": ((T, 2 * FEATS), F32), "s": ((T, T), F32),
        "tab": ((PAIRS, 2 * LANES, 2 * FEATS), BF), "tabn": ((PAIRS, LANES, 2 * FEATS), BF),
        "q": (pair, BF), "k": (pair, BF), "v": (pair, BF), "rb": (pair, F32),
        "qf": ((HEADS, T, 2 * FEATS), BF), "kf": ((HEADS, T, 2 * FEATS), BF),
        "out": (STATES, F32), "inn": (STATES, F32), "adj": (STATES, F32), "aend": (STATES, F32),
        "w": ((HEADS, T, T), BF), "own": ((HEADS, T, LANES), F32), "joined": ((HEADS, T, LANES), F32),
        "att": (pair, BF), "zfix": (pair, BF), "mid": ((T, D), F32), "xhat": ((T, D), F32), "inv": ((T, LANES), F32), "two": ((T, D), BF),
        "acc1": ((T, D), F32), "acc2": ((T, D), F32), "h1": ((T, ff), F32), "h2": ((T, ff), F32),
        "act": ((PAIRS, T, ff), BF), "gh": ((PAIRS, T, ff), BF), "sums": ((16, D), F32), "fsum": ((8, D), F32),
        "result": ((T, D), BF), "gmid": ((T, D), F32), "gb": ((T, D), BF), "dr": ((8, T), F32),
        "dn": ((HEADS, T, LANES), BF), "ds": ((T, T), BF), "da": ((PAIRS, T, 4 * FEATS), BF), "ghv": ((HEADS, T, LANES), F32),
        "lines": ((PAIRS, D // LANES, 8, LANES), F32),
        "drun": ((8, T), F32), "owed": ((8, LANES), F32), "gtok": ((T, D), F32),
    }


FRONT = (
    ("ga",),
    ("gate", "vec", "normed", "logits", "run", "total", "mask", "tabn", "q", "k", "v", "rb", "qf", "kf", "out", "w", "own", "zfix"),
    ("bias", "s1", "s2", "s", "tab"),
)
MIDDLE = (
    ("gf", "vec", "rb", "qf", "own", "zfix", "inn", "total"),
    ("ggf", "result", "gmid", "fsum", "dr", "dn", "adj"),
    ("joined", "att", "mid", "xhat", "inv", "two", "acc1", "acc2", "h1", "h2", "act", "gh", "sums", "gb"),
)
BACK = (
    ("ga", "gate", "vec", "normed", "logits", "run", "total", "mask", "tabn", "q", "k", "v", "rb", "qf", "kf",
     "w", "inn", "aend", "gmid", "fsum", "dr", "dn"),
    ("gga", "gtok", "lines"),
    ("s", "s1", "s2", "ds", "da", "ghv", "drun", "owed", "acc1", "sums"),
)
SHARED = {"joined": "own", "h1": "s", "gmid": "mid", "ds": "gb", "adj": "out", "da": "act", "ghv": "own"}


def front(T, base, r):
    tables(T, base, r)
    first_norm(T, base, r)
    keys(T, base, r)
    queries(T, base, r)


def middle(T, base, r):
    attend(T, base, r)
    feed(T, base, r)
    feed_grads(T, base, r)


def here(T):
    return (lax.axis_index("seq") * lax.axis_size("head") + lax.axis_index("head")) * T


def stage(which, names, specs, outer, args, state):
    reads, writes, scratch = names
    shape = lambda n: jax.ShapeDtypeStruct(*specs[n])
    vmem, smem = pl.BlockSpec(memory_space=pltpu.VMEM), pl.BlockSpec(memory_space=pltpu.SMEM)

    def kernel(*refs):
        base_ref, lengths, seed, tok, cot = refs[:5]
        rest = dict(zip(reads + writes + scratch, refs[5:]))
        which(base_ref[0], Refs(lengths=lengths, seed=seed, tok=tok, cot=cot, **rest))

    out = pl.pallas_call(
        kernel,
        out_shape=[shape(n) for n in writes],
        in_specs=[smem] * 3 + [vmem] * (2 + len(reads)),
        out_specs=[vmem] * len(writes),
        scratch_shapes=[pltpu.VMEM(*specs[n]) for n in scratch],
        compiler_params=pltpu.CompilerParams(vmem_limit_bytes=VMEM_BYTES),
        name=outer,
    )(*args, *[state[n] for n in reads])
    state.update(zip(writes, out))


def scan_states(out, reverse):
    seq, head = lax.axis_size("seq"), lax.axis_size("head")
    count = seq * head
    me = lax.axis_index("seq") * head + lax.axis_index("head")
    state = (out[:, DECAY : DECAY + 1, 0:1], out[:, :DECAY])
    step = 1
    order = lambda pairs: [(b, a) for a, b in pairs] if reverse else pairs
    axes = ("seq", "head")
    while step < count:
        moved = jax.tree.map(lambda x: lax.ppermute(x, axes, order([(i, i + step) for i in range(count - step)])), state)
        has = (me < count - step) if reverse else (me >= step)
        f, m = state
        state = (jnp.where(has, f * moved[0], f), m + jnp.where(has, f * moved[1], 0.0))
        step *= 2
    moved = lax.ppermute(state[1], axes, order([(i, i + 1) for i in range(count - 1)]))
    return jnp.concatenate([moved, jnp.zeros((HEADS, STATE_ROWS - DECAY, 2 * FEATS), F32)], axis=1)


def remote(src, dst, send, recv, to):
    return pltpu.make_async_remote_copy(
        src_ref=src, dst_ref=dst, send_sem=send, recv_sem=recv, device_id=to, device_id_type=MESH
    )


class Place:
    def __init__(self):
        self.seq, self.head = lax.axis_size("seq"), lax.axis_size("head")
        s, h = lax.axis_index("seq"), lax.axis_index("head")
        self.z, self.y, self.x, self.c = s // 2, s % 2, h // 2, h % 2
        self.depth = self.seq // 2
        self.count = self.seq * self.head
        self.me = s * self.head + h

    def device(self, z=None, y=None, x=None, c=None):
        pick = lambda given, own: own if given is None else given
        z, y, x, c = pick(z, self.z), pick(y, self.y), pick(x, self.x), pick(c, self.c)
        return (z * 2 + y, x * 2 + c)

    def number(self, i):
        return (i // self.head, i % self.head)

    def around(self, k):
        return (self.z + k) % self.depth

class Semaphores:
    def __init__(self, send, recv):
        self.send, self.recv, self.used = send, recv, 0

    def copy(self, src, dst, to):
        i = self.used
        self.used += 1
        return remote(src, dst, self.send.at[i], self.recv.at[i], to)


GATHER_COPIES = 2 * (3 + 1 + 2 + 2)
SCATTER_COPIES = 2 + 2 * (1 + 1 + 3)


def gather_stages(place, g, lanes, sems):
    half = g.shape[3] // 2
    z, y, x, c = place.z, place.y, place.x, place.c
    pair = x * 2 + c
    stages = [[], [], [], []]
    for part in range(2):
        rows = pl.ds(part * half, half)
        same = lambda ref, to: sems.copy(ref, ref, to)
        for k in range(1, place.depth):
            stages[0].append(same(g.at[pair, z, y, rows, lanes], place.device(z=place.around(k))))
        to_y, to_x = place.device(y=1 - y), place.device(x=1 - x)
        if part == 0:
            stages[1].append(same(g.at[pair, :, y, rows, lanes], to_y))
            stages[2].append(same(g.at[pair, :, :, rows, lanes], to_x))
        else:
            stages[1].append(same(g.at[pair, :, y, rows, lanes], to_x))
            for other in range(2):
                stages[2].append(same(g.at[other * 2 + c, :, y, rows, lanes], to_y))
        for other in range(2):
            stages[3].append(same(g.at[other * 2 + c, :, :, rows, lanes], place.device(c=1 - c)))
    return stages


def begin(stage):
    for copy in stage:
        copy.start()


def arrived(stage):
    for copy in stage:
        copy.wait_recv()


def sent(*stages):
    for stage in stages:
        for copy in stage:
            copy.wait_send()


class Gather:
    def __init__(self, place, ga, gf, sems):
        ff = (gf.shape[-1] - LANES) // 2
        lanes = lambda first, count: pl.ds(first, count)
        self.chunks = [
            gather_stages(place, ref, part, sems)
            for ref, part in (
                (ga, lanes(0, 3 * LANES)),
                (ga, lanes(3 * LANES, LANES)),
                (gf, lanes(0, LANES + ff)),
                (gf, lanes(LANES + ff, ff)),
            )
        ]

    def begin(self, chunk):
        begin(self.chunks[chunk][0])

    def step(self, chunk, stage):
        arrived(self.chunks[chunk][stage])
        if stage < 3:
            begin(self.chunks[chunk][stage + 1])

    def finish(self):
        for chunk in self.chunks:
            sent(*chunk)


def add_blocks(to, others, count, where):
    def one(i, carry):
        at = where(i)
        total = to[at].astype(F32)
        for ref, index in others:
            total = total + ref[index(i)].astype(F32)
        to[at] = total.astype(to.dtype)
        return carry

    lax.fori_loop(0, count, one, 0)


class Scatter:
    def __init__(self, place, gg, out, buf, sems):
        self.place, self.gg, self.out = place, gg, out
        self.r1, self.r2a, self.r2b, self.r3a, self.r3b, self.r4a, self.r4b = buf
        z, y, x, c, n = place.z, place.y, place.x, place.c, place.depth
        self.half = half = gg.shape[3] // 2
        first, last = pl.ds(0, half), pl.ds(half, half)
        other, to_y, to_x = place.device(c=1 - c), place.device(y=1 - y), place.device(x=1 - x)
        self.stages = [
            [sems.copy(gg.at[i * 2 + 1 - c], self.r1.at[i], other) for i in range(2)],
            [
                sems.copy(self.r1.at[1 - x, :, :, first], self.r2a, to_x),
                sems.copy(self.r1.at[:, :, 1 - y, last], self.r2b, to_y),
            ],
            [sems.copy(self.r2a.at[:, 1 - y], self.r3a, to_y), sems.copy(self.r2b.at[1 - x], self.r3b, to_x)],
            [
                sems.copy(ref.at[place.around(k)], slots.at[k - 1], place.device(z=place.around(k)))
                for ref, slots in ((self.r3a, self.r4a), (self.r3b, self.r4b))
                for k in range(1, n)
            ],
        ]

    def start(self):
        begin(self.stages[0])

    def step(self, i):
        place, n, half = self.place, self.place.depth, self.half
        y, x, c = place.y, place.x, place.c
        first, last = slice(0, half), slice(half, 2 * half)
        arrived(self.stages[i])
        if i == 0:
            block = lambda j: (j // (2 * n), (j // 2) % n, j % 2)
            add_blocks(self.r1, [(self.gg, lambda j: ((j // (2 * n)) * 2 + c, (j // 2) % n, j % 2))], 4 * n, block)
        elif i == 1:
            add_blocks(self.r2a, [(self.r1, lambda j: (x, j // 2, j % 2, first))], 2 * n, lambda j: (j // 2, j % 2))
            add_blocks(self.r2b, [(self.r1, lambda j: (j // n, j % n, y, last))], 2 * n, lambda j: (j // n, j % n))
        elif i == 2:
            add_blocks(self.r3a, [(self.r2a, lambda j: (j, y))], n, lambda j: (j,))
            add_blocks(self.r3b, [(self.r2b, lambda j: (x, j))], n, lambda j: (j,))
        else:
            for ref, slots, rows in ((self.r3a, self.r4a, first), (self.r3b, self.r4b, last)):
                total = ref[place.z].astype(F32)
                for k in range(n - 1):
                    total = total + slots[k].astype(F32)
                self.out[rows, :] = total
        if i < 3:
            begin(self.stages[i + 1])

    def finish(self):
        sent(*self.stages)


def scatter_buffers(seq, rows, cols):
    n, half = seq // 2, rows // 2
    return [
        pltpu.VMEM(shape + (cols,), BF)
        for shape in ((2, n, 2, rows), (n, 2, half), (2, n, half), (n, half), (n, half), (n - 1, half), (n - 1, half))
    ]


class Scan:
    def __init__(self, place, reverse, out, inn, box, planes, send, recv):
        self.place, self.reverse = place, reverse
        self.out, self.inn, self.box, self.planes = out, inn, box, planes
        self.send, self.recv = send, recv
        self.mine = lax.rem(place.me, HEADS)

    def device(self, j):
        return self.place.number(self.place.me - self.mine + j)

    def peers(self, body):
        def one(k, carry):
            body(lax.rem(self.mine + k, HEADS))
            return carry

        lax.fori_loop(1, HEADS, one, 0)

    def all_at_once(self, ref, count, i):
        most = ref.at[pl.ds(0, count)]
        return remote(most, most, self.send.at[i], self.recv.at[i], self.place.device(c=1 - self.place.c))

    def start(self):
        me = self.mine
        self.peers(lambda j: remote(self.out.at[j], self.box.at[me], self.send.at[0], self.recv.at[0], self.device(j)).start())
        self.box[me] = self.out[me]

    def chain(self, ref, count):
        kept = iota((STATE_ROWS, 2 * FEATS), 0) != DECAY

        def one(i, state):
            d = count - 1 - i if self.reverse else i
            term = ref[d]
            ref[d] = state
            return state * term[DECAY : DECAY + 1, :] + jnp.where(kept, term, 0.0)

        first = jnp.where(iota((STATE_ROWS, 2 * FEATS), 0) == DECAY, 1.0, 0.0)
        return lax.fori_loop(0, count, one, first)

    def plane(self):
        place = self.place
        self.all_at_once(self.box, HEADS - 1, 0).wait_recv()
        self.planes[place.z] = self.chain(self.box, HEADS)
        for copy in self.totals():
            copy.start()

    def totals(self):
        place = self.place
        total = self.planes.at[place.z]
        return [
            remote(total, total, self.send.at[1], self.recv.at[1], place.device(z=place.around(k)))
            for k in range(1, place.depth)
        ]

    def line(self):
        place, me = self.place, self.mine
        self.all_at_once(self.planes, place.depth - 1, 1).wait_recv()
        self.all_at_once(self.planes, place.depth - 1, 1).wait_send()
        self.chain(self.planes, place.depth)
        before = self.planes[place.z]

        def one(j, carry):
            own = self.box[j]
            self.box[j] = own + own[DECAY : DECAY + 1, :] * before
            return carry

        lax.fori_loop(0, HEADS, one, 0)
        self.peers(lambda j: remote(self.box.at[j], self.inn.at[me], self.send.at[2], self.recv.at[2], self.device(j)).start())
        self.inn[me] = self.box[me]

    def receive(self):
        self.all_at_once(self.inn, HEADS - 1, 2).wait_recv()

    def finish(self):
        self.all_at_once(self.out, HEADS - 1, 0).wait_send()
        self.all_at_once(self.box, HEADS - 1, 2).wait_send()


class Lines:
    def __init__(self, place, lines, box, out, send, recv):
        self.place, self.lines, self.box, self.out, self.send, self.recv = place, lines, box, out, send, recv

    def tile(self, j):
        return self.lines.at[lax.rem(j, self.place.head), (j // self.place.head) * self.lines.shape[1] // self.place.seq]

    def start(self):
        me, count = self.place.me, self.place.count

        def one(k, carry):
            j = lax.rem(me + k, count)
            remote(self.tile(j), self.box.at[me], self.send, self.recv, self.place.number(j)).start()
            return carry

        lax.fori_loop(1, count, one, 0)
        self.box[me] = self.tile(me)[...]

    def finish(self):
        most = self.box.at[pl.ds(0, self.place.count - 1)]
        both = remote(most, most, self.send, self.recv, self.place.device(c=1 - self.place.c))
        both.wait_recv()

        def one(i, total):
            return total + self.box[i]

        self.out[...] = lax.fori_loop(0, self.place.count, one, jnp.zeros(self.out.shape, F32))
        both.wait_send()


def greet_all(place):
    barrier = pltpu.get_barrier_semaphore()

    def one(k, carry):
        to = place.number(lax.rem(place.me + k, place.count))
        pl.semaphore_signal(barrier, inc=1, device_id=to, device_id_type=MESH)
        return carry

    lax.fori_loop(1, place.count, one, 0)
    pl.semaphore_wait(barrier, place.count - 1)


def layer_kernel(names, specs, tokens_all, T, lengths, seed, tok, cot, att, rest, result, gtok, grad_a, grad_f, grad_lines, *scratch):
    place = Place()
    base = place.me * T
    arrays = dict(zip(names, scratch))
    arrays.update({name: arrays[other] for name, other in SHARED.items()})
    scratch = scratch[len(names) :]
    r = Refs(lengths=lengths, seed=seed, tok=tok, cot=cot, result=result, gtok=gtok, **arrays)
    scatter_f, scatter_a, scratch = scratch[0:7], scratch[7:14], scratch[14:]
    box, planes, line_box, sems = scratch[0:2], scratch[2:4], scratch[4], scratch[5:]
    pair = place.x * 2 + place.c
    r.ga[pair, place.z, place.y] = att[...]
    r.gf[pair, place.z, place.y] = rest[...]
    gather = Gather(place, r.ga, r.gf, Semaphores(sems[0], sems[1]))
    forth = Scan(place, False, r.out, r.inn, box[0], planes[0], sems[2], sems[3])
    home = Scan(place, True, r.adj, r.aend, box[1], planes[1], sems[4], sems[5])
    later = Semaphores(sems[6], sems[7])
    sum_f = Scatter(place, r.ggf, grad_f, scatter_f, later)
    sum_a = Scatter(place, r.gga, grad_a, scatter_a, later)
    lines = Lines(place, r.lines, line_box, grad_lines, sems[8], sems[9])
    greet_all(place)

    def acts(*each):
        def run():
            for act, *given in each:
                act(*given)

        return run

    gather.begin(0)
    gather.begin(1)
    tables(T, base, r)
    acts((gather.step, 0, 0), (gather.begin, 2), (gather.step, 0, 1), (gather.step, 1, 0), (gather.step, 0, 2),
         (gather.step, 1, 1), (gather.step, 0, 3))()
    first_norm(T, base, r)
    acts((gather.step, 1, 2), (gather.step, 2, 0), (gather.begin, 3))()
    keys(T, base, r, {1: acts((gather.step, 2, 1)), 2: acts((gather.step, 1, 3))})
    forth.start()
    queries(T, base, r, {0: acts((gather.step, 2, 2), (gather.step, 3, 0)), 1: acts((forth.plane,), (gather.step, 3, 1)),
                         2: acts((forth.line,), (gather.step, 2, 3), (gather.step, 3, 2))})
    forth.receive()
    forth.finish()
    attend(T, base, r)
    gather.step(3, 3)
    feed(T, base, r)
    home.start()
    feed_grads(T, base, r, {1: home.plane})
    sum_f.start()
    back(T, base, r, tokens_all, {0: home.line, 2: acts((sum_f.step, 0))}, home.receive,
         {0: acts((sum_f.step, 1)), 2: acts((sum_f.step, 2))})
    lines.start()
    sum_a.start()
    sum_f.step(3)
    for i in range(3):
        sum_a.step(i)
    lines.finish()
    sum_a.step(3)
    gather.finish()
    home.finish()
    sum_f.finish()
    sum_a.finish()


def layer_near(lengths, seed, tokens, cotangent, att, rest, specs, seq, head):
    T, D = tokens.shape
    count = seq * head
    rows, ff = D // seq, specs["act"][0][2]
    held = [n for n in dict.fromkeys(sum((sum(names, ()) for names in (FRONT, MIDDLE, BACK)), ())) if n not in SHARED]
    held = [n for n in held if n not in ("result", "gtok")]
    dma = pltpu.SemaphoreType.DMA
    scratch = [pltpu.VMEM(*specs[n]) for n in held]
    panels = att.shape[1] - LANES
    scratch += scatter_buffers(seq, rows, rest.shape[1]) + scatter_buffers(seq, rows, panels)
    scratch += [pltpu.VMEM(STATES, F32)] * 2 + [pltpu.VMEM((seq // 2,) + STATES[1:], F32)] * 2
    scratch += [pltpu.VMEM((count, 8, LANES), F32)]
    scratch += [dma((4 * GATHER_COPIES,))] * 2 + [dma((3,))] * 4 + [dma((2 * SCATTER_COPIES,))] * 2 + [dma(())] * 2
    vmem, smem = pl.BlockSpec(memory_space=pltpu.VMEM), pl.BlockSpec(memory_space=pltpu.SMEM)
    shape = jax.ShapeDtypeStruct
    return pl.pallas_call(
        functools.partial(layer_kernel, held, specs, T * count, T),
        out_shape=[shape((T, D), BF), shape((T, D), F32), shape((rows, panels), F32), shape((rows, rest.shape[1]), F32),
                   shape((8, LANES), F32)],
        in_specs=[smem] * 2 + [vmem] * 4,
        out_specs=[vmem] * 5,
        scratch_shapes=scratch,
        compiler_params=pltpu.CompilerParams(collective_id=0, has_side_effects=True, vmem_limit_bytes=LAYER_BYTES),
        name="layer",
    )(lengths, seed, tokens, cotangent, att, rest)


def bias_columns(gate_bias):
    hi = lax.reduce_precision(gate_bias, 8, 7)
    mid = lax.reduce_precision(gate_bias - hi, 8, 7)
    return jnp.stack([hi, mid, gate_bias - hi - mid], axis=1).astype(BF)


def gather_any(q, k, v, gate, vectors, bias, out, up, down, seq):
    D = q.shape[0] * seq

    def whole(w, rows, cols):
        w = lax.all_gather(w, rows, axis=0, tiled=True)
        return lax.all_gather(w, cols, axis=1, tiled=True)

    def panels(w):
        return w.reshape(D, PAIRS, w.shape[1] // PAIRS).transpose(1, 0, 2)

    q, k, v = (panels(whole(w, "seq", "head")) for w in (q, k, v))
    gates = panels(whole(gate, "seq", "head"))
    lines = [jnp.broadcast_to(lax.all_gather(w, "seq", tiled=True)[None, :, None], (PAIRS, D, 1)) for w in vectors]
    bias = bias_columns(lax.all_gather(bias, "head", tiled=True)).reshape(PAIRS, 1, 6)
    pad = jnp.zeros((PAIRS, D, LANES - 12), BF)
    ga = jnp.concatenate([k, v, gates] + lines + [jnp.broadcast_to(bias, (PAIRS, D, 6)), pad, q], axis=2)
    gf = [panels(whole(out, "head", "seq").T), panels(whole(up, "seq", "head")), panels(whole(down, "head", "seq").T)]
    gf = jnp.concatenate(gf, axis=2)
    shape = (PAIRS, seq // 2, 2, D // seq)
    return ga.reshape(shape + ga.shape[2:]), gf.reshape(shape + gf.shape[2:])


def unpack(grad_a, grad_f, lines, ff):
    rows = grad_a.shape[0]
    block = lambda i: grad_a[:, i * LANES : (i + 1) * LANES]
    place = lax.axis_index("seq") % (LANES // rows) * rows
    own = lax.dynamic_slice_in_dim(lines, place, rows, 1)
    return (
        own[2], own[3], block(2), block(0), block(1), own[0:2].T, lines[6:8, 0],
        grad_f[:, :LANES].T, own[4], own[5], grad_f[:, LANES : LANES + ff], grad_f[:, LANES + ff :].T,
    )


def scatter_any(gga, ggf, lines, ff):
    gga, ggf = (x.reshape(PAIRS, -1, x.shape[-1]).astype(F32) for x in (gga, ggf))

    def grid(x):
        x = x.transpose(1, 0, 2).reshape(x.shape[1], -1)
        x = lax.psum_scatter(x, "seq", scatter_dimension=0, tiled=True)
        return lax.psum_scatter(x, "head", scatter_dimension=1, tiled=True)

    block = lambda i: gga[:, :, i * LANES : (i + 1) * LANES]
    lines = lines.transpose(0, 2, 1, 3).reshape(PAIRS, 8, -1)
    gates = lines[:, 0:2].transpose(0, 2, 1)
    bias = lines[:, 6:8, 0].reshape(HEADS)
    bias = lax.psum_scatter(lax.psum(bias, "seq"), "head", scatter_dimension=0, tiled=True)
    lines = lax.psum_scatter(lax.psum(lines[0, 2:6].T, "head"), "seq", scatter_dimension=0, tiled=True)
    return (
        lines[:, 0], lines[:, 1], grid(block(2)), grid(block(0)), grid(block(1)), grid(gates), bias,
        grid(ggf[:, :, :LANES]).T, lines[:, 2], lines[:, 3], grid(ggf[:, :, LANES : LANES + ff]),
        grid(ggf[:, :, LANES + ff :]).T,
    )


def shards(
    tokens, lengths, feature_seed, norm_gain, norm_shift, query_weight, key_weight, value_weight, gate_weight, gate_bias,
    out_weight, ffn_gain, ffn_shift, up_weight, down_weight, cotangent,
):
    seq, head = lax.axis_size("seq"), lax.axis_size("head")
    T, D = tokens.shape
    rows = D // seq
    ff = up_weight.shape[1] * head // PAIRS
    vectors = (norm_gain, norm_shift, ffn_gain, ffn_shift)
    specs = buffers(T, D, ATT, LANES + 2 * ff, ff, seq)
    if (seq, head) == (HEADS, PAIRS):
        bias = jnp.broadcast_to(bias_columns(gate_bias).reshape(1, 6), (rows, 6))
        small = [gate_weight] + [w[:, None] for w in vectors] + [bias, jnp.zeros((rows, LANES - 12), BF)]
        att = jnp.concatenate([key_weight, value_weight] + small + [query_weight], axis=1)
        rest = jnp.concatenate([out_weight.T, up_weight, down_weight.T], axis=1)
        result, grad_tokens, grad_a, grad_f, lines = layer_near(
            lengths, feature_seed, tokens, cotangent, att, rest, specs, seq, head)
        return (result, grad_tokens) + unpack(grad_a, grad_f, lines, ff)
    ga, gf = gather_any(query_weight, key_weight, value_weight, gate_weight, vectors, gate_bias, out_weight, up_weight,
                        down_weight, seq)
    args = (here(T).astype(I32).reshape(1), lengths, feature_seed, tokens, cotangent)
    state = {"ga": ga, "gf": gf}
    stage(lambda base, r: front(T, base, r), FRONT, specs, "front", args, state)
    state["inn"] = scan_states(state["out"], False)
    stage(lambda base, r: middle(T, base, r), MIDDLE, specs, "middle", args, state)
    state["aend"] = scan_states(state["adj"], True)
    stage(lambda base, r: back(T, base, r, T * seq * head), BACK, specs, "back", args, state)
    return (state["result"], state["gtok"]) + scatter_any(state["gga"], state["ggf"], state["lines"], ff)


def solution(mesh):
    both, rows, grid = P(("seq", "head"), None), P("seq"), P("seq", "head")
    return jax.shard_map(
        shards,
        mesh=mesh,
        in_specs=(both, P(), P(), rows, rows, grid, grid, grid, grid, P("head"), P("head", "seq"), rows, rows, grid,
                  P("head", "seq"), both),
        out_specs=(both, both, rows, rows, grid, grid, grid, grid, P("head"), P("head", "seq"), rows, rows, grid,
                   P("head", "seq")),
        check_vma=False,
    )
```

time: 669 us -> 187 us (0.28)
  waiting for transfers between devices: 377 us -> 0 us
  starting transfers between devices: 96.1 us -> 0 us
  Pallas kernels: 94.5 us -> 169 us
  blocking collectives: 36 us -> 0 us
  other arithmetic: 19.8 us -> 0.7 us
  between operations: 15.4 us -> 1.36 us
  local copies, waits for them, and re-layouts: 28.6 us -> 14.9 us
    reduce_scatter x3 -> x0, waiting for transfers between devices: 181 us -> none  [the longest x2 117 us: scattered(): x = lax.psum_scatter(x, 'head', scatter_dimension=0, tiled=True)[0]]
    ppermute x32 -> x0, waiting for transfers between devices: 100 us -> none  [the longest x28 97.6 us: scan_states(): lax.ppermute(x, axes, order([(i, i + step) for i in range(count - step)]))]
    ppermute x32 -> x0, starting transfers between devices: 95.8 us -> none  [the longest x28 90.5 us: scan_states(): lax.ppermute(x, axes, order([(i, i + step) for i in range(count - step)]))]
    pallas_call x3 -> x1, Pallas kernels: 94.5 us -> 169 us  [layer_near(): pl.pallas_call(functools.partial(layer_kernel, held, specs, T * count, T)...]
    unnamed x8 -> x0, waiting for transfers between devices: 67.2 us -> none
    all_gather x1 -> x0, blocking collectives: 36 us -> none  [gather(): lax.all_gather(block, 'seq', axis=0, tiled=True)]
    all_gather x3 -> x0, waiting for transfers between devices: 29 us -> none  [the longest x2 22.1 us: gather(): lax.all_gather(lax.all_gather(block, 'seq', axis=0, tiled=True), 'head',...]
    convert_element_type x6 -> x0, other arithmetic: 13 us -> none  [the longest x2 11 us: scattered(): x = x.reshape(PAIRS, -1, x.shape[-1]).astype(F32)]
  transfers between devices with their start and end apart: 39 -> 0, of which waited for: 25 -> 0; matrix products, arithmetic and copies ran while one was open for 5% -> 0% of each run, Pallas kernels for 5% -> 0%
where the time goes in v2:
time: 187 us; the launch traced here: 186 us
  Pallas kernels  169 us (90%)
  local copies, waits for them, and re-layouts  14.9 us (8%)
    pallas_call x1, Pallas kernels, layer_near(): pl.pallas_call(functools.partial(layer_kernel, held, specs, T * count, T)...  169 us
    unnamed x29, local copies, waits for them, and re-layouts  7.16 us

profile of v2, /device:TPU:0, one launch (start us, length us, event | category | flops | bytes accessed | tf_op | source)
XLA Modules:
  0.0 186.4 jit_solution(10500474711980917451)
XLA Ops:
  1.3 0.0 copy-start.12
  1.3 0.6 copy-done.12
  2.0 0.1 copy.36
  2.1 0.1 convert_element_type.8
  2.2 0.6 copy-done.7
  2.8 0.1 copy.38
  3.0 0.5 copy-done.8
  3.5 0.1 copy.39
  3.6 0.5 copy-done.9
  4.2 0.1 copy.37
  4.3 0.5 copy-done.10
  4.8 0.1 copy.40
  4.9 0.5 copy-done.11
  5.5 0.1 copy.41
  5.6 0.0 copy-done.5
  5.6 0.6 copy-done.3
  6.2 0.0 copy-done.4
  6.2 0.7 concatenate.6.att
  6.9 0.1 copy-done.1
  7.0 0.0 copy-done.2
  7.1 0.0 copy-done.6
  7.1 0.7 pad_maximum_fusion.rest
  7.7 169.4 %layer.1 = (bf16[512,512]{1,0:T(8,128)(2,1)}, f32[512,512]{1,0:T(8,128)}, f32[64,384]{1,0:T(8,128)}, f32[64,1152]{1,0:T(8,128)}, f32[8,128]{1,0:T(8,128)}) custom-call(s32[3]{0:T(128)} %lengths.1, s32[1]{0:T(128)S(6)} %copy.44.seed, bf16[512,512]{1,0:T(8,128)(2,1)} %tok.1, bf16[512,512]{1,0:T(8,128)(2,1)} %cot.1, bf16[64,512]{1,0:T(8,128)(2,1)} %concatenate.6.att, ...), custom_call_target="tpu_custom_call" | custom-call | tf_op jit(solution)/shard_map/layer/pallas_call | solution.py:1058
  177.1 0.0 copy-start
  177.1 1.4 slice_reduce_fusion
  178.5 0.8 constant_dynamic-slice_fusion
  179.3 0.6 slice_bitcast_fusion.2
  179.9 0.5 slice_bitcast_fusion.3
  180.4 1.5 fusion.4
  181.8 1.7 slice_bitcast_fusion
  183.5 1.9 %copy.45 = bf16[512,512]{1,0:T(8,128)(2,1)} copy(bf16[512,512]{1,0:T(8,128)(2,1)} %get-tuple-element.51) | data formatting | bytes 1048576
  185.4 1.0 copy.46
  (16 shorter events, 0.0 us)
Async XLA Ops:
  1.3 0.7 copy-start.12
  2.2 0.7 copy-start.7
  2.8 0.7 copy-start.8
  3.5 0.7 copy-start.9
  4.1 0.7 copy-start.10
  4.8 0.7 copy-start.11
  4.8 0.8 copy-start.5
  5.5 0.7 copy-start.3
  5.5 0.7 copy-start.4
  6.2 0.8 copy-start.1
  6.2 0.9 copy-start.2
  6.2 0.9 copy-start.6
  177.1 8.3 %copy-start = (f32[512,512]{1,0:T(8,128)S(1)}, f32[512,512]{1,0:T(8,128)}, u32[]{:S(2)}) copy-start(f32[512,512]{1,0:T(8,128)} %get-tuple-element.52) | copy-start | bytes 3145732
